TPU v7x, 32 devices: a whole 2x2x4 slice. The times are simulated.
32 devices in a mesh: section: 4 (over y, core), dp: 8 (over z, x).
Axes of the slice: x: 2, y: 2, z: 4, core: 2. Of those that a mesh axis runs over, the one named last changes fastest.
Arguments:
- entry_states: bfloat16 [5, 256, 4608], P(None, 'dp'), may hold values from -6 to 6
- down_proj: bfloat16 [4, 4, 4608, 128], P('section'), may hold values from -0.09375 to 0.09375
- up_proj: bfloat16 [4, 4, 4608, 128], P('section'), may hold values from -0.5 to 0.5
- label_rows: bfloat16 [256, 4608], replicated, may hold values from -0.375 to 0.375
- sampled_labels: int32 [4, 5, 256], P(None, None, 'dp'), may hold values from 0 to 255
- eval_states: bfloat16 [256, 4608], P('dp'), may hold values from -6 to 6
Outputs:
- eval_out: bfloat16 [4, 256, 4608], P('section', 'dp')
- label_logprob: float32 [4, 5, 256], P('section', None, 'dp')
- fisher_log: float32 [4, 2, 4608, 128], P('section', None, 'dp')
All inputs are finite; a program needn't handle non-finite values.
Results may differ from a plain program's by a relative error of at most 0.0065.
Values may be sent and summed in bfloat16 or wider, within the bound.
No kernel may reach another device: no remote copies, remote signals or barrier semaphores. Data moves between devices by JAX's collectives and lax.ppermute only.
A program may use at most 128 MiB of HBM per device.

v0:
```python
import functools

import jax
import jax.numpy as jnp
from jax import lax
from jax.experimental import pallas as pl
from jax.experimental.pallas import tpu as pltpu
from jax.sharding import PartitionSpec as P

norm_eps = 1e-06
merge_eps = 1e-06
soft_cap = 30.0
gelu_coef = 0.7978845608028654
vmem_bytes = 56 * 1024 * 1024
bf16 = jnp.bfloat16
f32 = jnp.float32


def nt_dot(lhs, rhs):
    return lax.dot_general(lhs, rhs, (((1,), (1,)), ((), ())), preferred_element_type=f32)


def nn_dot(lhs, rhs):
    return lax.dot_general(lhs, rhs, (((1,), (0,)), ((), ())), preferred_element_type=f32)


def tn_dot(lhs, rhs):
    return lax.dot_general(lhs, rhs, (((0,), (0,)), ((), ())), preferred_element_type=f32)


def gelu_value(hidden):
    inner = gelu_coef * (hidden + 0.044715 * hidden * hidden * hidden)
    return 0.5 * hidden * (1.0 + jnp.tanh(inner))


def gelu_slope(hidden):
    inner = gelu_coef * (hidden + 0.044715 * hidden * hidden * hidden)
    tanh_value = jnp.tanh(inner)
    return 0.5 * (1.0 + tanh_value) + 0.5 * hidden * (1.0 - tanh_value * tanh_value) * gelu_coef * (
        1.0 + 3.0 * 0.044715 * hidden * hidden
    )


def row_scale(states):
    return lax.rsqrt(jnp.mean(states * states, axis=-1, keepdims=True) + norm_eps)


def square(values):
    wide = values.astype(f32)
    return (wide * wide).astype(bf16)


def label_head(states, labels, label_rows):
    wide = states.astype(f32)
    scale = row_scale(wide)
    norm_float = wide * scale
    logits = nt_dot(norm_float.astype(bf16), label_rows)
    bent = jnp.tanh(logits / soft_cap)
    capped = soft_cap * bent
    logprob = capped - jnp.log(jnp.sum(jnp.exp(capped), axis=-1, keepdims=True))
    one_hot = (labels == lax.broadcasted_iota(jnp.int32, logprob.shape, 1)).astype(f32)
    picked = jnp.sum(logprob * one_hot, axis=-1, keepdims=True)
    slope = ((jnp.exp(logprob) - one_hot) * (1.0 - bent * bent)).astype(bf16)
    grad_norm = nn_dot(slope, label_rows)
    mean = jnp.mean(grad_norm * norm_float, axis=-1, keepdims=True)
    return (scale * (grad_norm - norm_float * mean)).astype(bf16), picked


class Copies:
    def __init__(self, sems):
        self.sems, self.used = sems, 0

    def start(self, source, target):
        copy = pltpu.make_async_copy(source, target, self.sems.at[self.used])
        self.used += 1
        copy.start()
        return copy


class StageWeights:
    def __init__(self, member, own, other, held, sems):
        self.member, self.own, self.other = member, own, other
        self.held, self.sems = held, sems
        self.tasks = held[0].shape[1]

    def copy(self, kind, layer, task):
        return pltpu.make_async_copy(
            self.other[kind].at[task], self.held[kind].at[layer, task], self.sems.at[kind, layer, task]
        )

    def start(self, order):
        for kind, layer in order:
            @pl.when(self.member == layer)
            def _():
                for task in range(self.tasks):
                    pltpu.make_async_copy(
                        self.own[kind].at[layer * self.tasks + task],
                        self.held[kind].at[layer, task],
                        self.sems.at[kind, layer, task],
                    ).start()

            @pl.when(self.member != layer)
            def _():
                for task in range(self.tasks):
                    self.copy(kind, layer, task).start()

    def get(self, kind, layer):
        for task in range(self.tasks):
            self.copy(kind, layer, task).wait()
        return [self.held[kind].at[layer, task] for task in range(self.tasks)]


def forward_layers(states, w_down, w_up):
    wide = [x.astype(f32) for x in states]
    normed = [(x * row_scale(x)).astype(bf16) for x in wide]
    hidden = [nn_dot(n, w[...]) for n, w in zip(normed, w_down())]
    active = [gelu_value(h).astype(bf16) for h in hidden]
    update = [nt_dot(a, w[...]) for a, w in zip(active, w_up())]
    return [(x + u).astype(bf16) for x, u in zip(wide, update)], hidden


def backward_layers(grads, states, hidden, w_down, w_up, keep):
    grad_act = [nn_dot(g, w[...]) for g, w in zip(grads, w_up())]
    grad_hidden = [(g * gelu_slope(h)).astype(bf16) for g, h in zip(grad_act, hidden)]
    scales, norms = [], []
    for task, states_task in enumerate(states):
        wide = states_task.astype(f32)
        scales.append(row_scale(wide))
        norms.append(wide * scales[task])
        keep(0, task, square(norms[task].astype(bf16)), square(grad_hidden[task]))
        keep(1, task, square(grads[task]), square(gelu_value(hidden[task]).astype(bf16)))
    if w_down is None:
        return None
    grad_norm = [nt_dot(g, w[...]) for g, w in zip(grad_hidden, w_down())]
    result = []
    for g, s, n, gn in zip(grads, scales, norms, grad_norm):
        mean = jnp.mean(gn * n, axis=-1, keepdims=True)
        result.append((g.astype(f32) + s * (gn - n * mean)).astype(bf16))
    return result


def square_keeper(copies, waits, layer, wide, narrow, wide_out, narrow_out):
    def keep(kind, task, wide_value, narrow_value):
        wide[layer, kind, task] = wide_value
        narrow[layer, kind, task] = narrow_value
        waits.append(copies.start(wide.at[layer, kind, task], wide_out.at[layer, kind, task]))
        waits.append(copies.start(narrow.at[layer, kind, task], narrow_out.at[layer, kind, task]))

    return keep


def first_forward_kernel(place, entry, down, up, down_other, up_other, out, middle, hidden,
                         base, mid, top, pre, sems, held_down, held_up, weight_sems):
    @pl.when(place[0] == 0)
    def _():
        tasks = out.shape[0]
        copies, waits = Copies(sems), []
        loaded = copies.start(entry.at[place[2]], base)
        weights = StageWeights(place[1], (down, up), (down_other, up_other), (held_down, held_up), weight_sems)
        weights.start([(0, 0), (1, 0), (0, 1), (1, 1)])
        loaded.wait()
        current = [base[...]] * tasks
        for layer in range(2):
            current, made = forward_layers(
                current, lambda: weights.get(0, layer), lambda: weights.get(1, layer)
            )
            held, target = (mid, middle) if layer == 0 else (top, out)
            for task in range(tasks):
                held[task] = current[task]
                waits.append(copies.start(held.at[task], target.at[task]))
                pre[layer, task] = made[task]
        waits.append(copies.start(pre, hidden))
        for copy in waits:
            copy.wait()


def first_backward_kernel(place, grad, entry, middle, hidden, down, up, down_other, up_other,
                          wide_out, narrow_out, grads, base, mid, pre, wide, narrow, sems,
                          held_down, held_up, weight_sems):
    @pl.when(place[0] == 0)
    def _():
        tasks = middle.shape[0]
        copies, waits = Copies(sems), []
        loads = [
            copies.start(source, target)
            for source, target in ((grad, grads), (hidden, pre), (middle, mid), (entry.at[place[2]], base))
        ]
        weights = StageWeights(place[1], (down, up), (down_other, up_other), (held_down, held_up), weight_sems)
        weights.start([(1, 1), (0, 1), (1, 0)])
        for load in loads:
            load.wait()
        current = [grads[task] for task in range(tasks)]
        for layer in (1, 0):
            states = [mid[task] if layer == 1 else base[...] for task in range(tasks)]
            current = backward_layers(
                current, states, [pre[layer, task] for task in range(tasks)],
                (lambda: weights.get(0, layer)) if layer == 1 else None,
                lambda: weights.get(1, layer),
                square_keeper(copies, waits, layer, wide, narrow, wide_out, narrow_out),
            )
        for copy in waits:
            copy.wait()


def last_stage_kernel(place, states, labels, label_rows, down, up, down_other, up_other,
                      grad_out, picked, wide_out, narrow_out,
                      base, mid, tops, words, marks, chosen, grads, wide, narrow, sems,
                      held_down, held_up, weight_sems):
    @pl.when(place[0] == 1)
    def _():
        tasks, rows = states.shape[0], states.shape[1]
        copies, waits = Copies(sems), []
        loaded = copies.start(states, base)
        weights = StageWeights(place[1], (down, up), (down_other, up_other), (held_down, held_up), weight_sems)
        weights.start([(0, 0), (1, 0), (0, 1), (1, 1)])
        later = [copies.start(label_rows, words), copies.start(labels.at[place[2]], marks)]
        loaded.wait()
        current = [base[task] for task in range(tasks)]
        hidden, down_refs, up_refs = [], [], []
        for layer in range(2):
            def take_down():
                down_refs.append(weights.get(0, layer))
                return down_refs[-1]

            def take_up():
                up_refs.append(weights.get(1, layer))
                return up_refs[-1]

            current, made = forward_layers(current, take_down, take_up)
            hidden.append(made)
            for task in range(tasks):
                if layer == 0:
                    mid[task] = current[task]
                else:
                    tops[task * rows:(task + 1) * rows] = current[task]
        for copy in later:
            copy.wait()
        grad, chosen[...] = label_head(tops[...], marks[...], words[...])
        waits.append(copies.start(chosen, picked))
        current = [grad[task * rows:(task + 1) * rows] for task in range(tasks)]
        for layer in (1, 0):
            below = [mid[task] if layer == 1 else base[task] for task in range(tasks)]
            current = backward_layers(
                current, below, hidden[layer],
                lambda: down_refs[layer], lambda: up_refs[layer],
                square_keeper(copies, waits, layer, wide, narrow, wide_out, narrow_out),
            )
        for task in range(tasks):
            grads[task] = current[task]
            waits.append(copies.start(grads.at[task], grad_out.at[task]))
        for copy in waits:
            copy.wait()


def eval_kernel(step, where, states, before, *refs):
    *pieces, out, base, top, held, sems = refs
    copies = Copies(sems)
    rows = pieces[0].shape[1]

    @pl.when(where[0] == step)
    def _():
        loads = [[copies.start(states, base)], [], []]
        for kind in range(2):
            for index, piece in enumerate(pieces):
                spot = pl.ds(pl.multiple_of(where[1 + index] * rows, 16), rows)
                loads[1 + kind].append(copies.start(piece.at[kind], held.at[kind, spot]))
        for load in loads[0]:
            load.wait()
        wide = base[...].astype(f32)
        normed = (wide * row_scale(wide)).astype(bf16)
        for load in loads[1]:
            load.wait()
        active = gelu_value(nn_dot(normed, held[0])).astype(bf16)
        for load in loads[2]:
            load.wait()
        top[...] = (wide + nt_dot(active, held[1])).astype(bf16)
        copies.start(top, out).wait()

    @pl.when(where[0] != step)
    def _():
        copies.start(before, base).wait()
        copies.start(base, out).wait()


def fisher_kernel(turns, place, *refs):
    wides, narrows = refs[:turns], refs[turns:2 * turns]
    own = refs[2 * turns:2 * turns + 2]
    other = refs[2 * turns + 2:2 * turns + 4]
    outs = refs[2 * turns + 4:]
    member = place[1]
    tasks = own[0].shape[0]
    for slot in range(2):
        layer = member if slot == 0 else 1 - member
        weights = own if slot == 0 else other
        for kind in range(2):
            top, total = None, None
            for task in range(tasks):
                left = jnp.concatenate([ref[layer, kind, task] for ref in wides], axis=0)
                right = jnp.concatenate([ref[layer, kind, task] for ref in narrows], axis=0)
                term = tn_dot(left, right)
                scaled = term * weights[kind][task].astype(f32)
                top = scaled if top is None else top + scaled
                total = term if total is None else total + term
            outs[slot][0, kind] = top.astype(outs[slot].dtype)
            outs[slot][1, kind] = total.astype(outs[slot].dtype)


def block_size(width):
    return max(size for size in range(128, 513, 128) if width % size == 0)


smem = pl.BlockSpec(memory_space=pltpu.SMEM)
hbm = pl.BlockSpec(memory_space=pl.ANY)


def send(block, axis, route):
    return lax.ppermute(block, axis, route)


def ring_order(count):
    if count % 2:
        return list(range(count))
    return list(range(0, count, 2)) + list(range(count - 1, 0, -2))


def ring_place(axis):
    count = lax.axis_size(axis)
    order = ring_order(count)
    spots = [order.index(device) for device in range(count)]
    spot = jnp.array(spots, jnp.int32)[lax.axis_index(axis)]
    table = jnp.array(order, jnp.int32)

    def block_at(offset):
        return table[lax.rem(spot + offset + 2 * count, count)]

    ahead = [(order[i], order[(i + 1) % count]) for i in range(count)]
    back = [(j, i) for i, j in ahead]
    return count, block_at, ahead, back


def ring_scatter(own, other, axis):
    count, block_at, ahead, back = ring_place(axis)
    rows = own.shape[2] // count

    def part(index, block):
        return sum(
            lax.dynamic_slice_in_dim(array[index], block * rows, rows, 1).astype(f32) for array in (own, other)
        )

    moving = [part(0, block_at(-1)).astype(bf16), part(1, block_at(1)).astype(bf16)]
    for step in range(count - 1):
        last = step == count - 2
        landed = [send(moving[0], axis, ahead), send(moving[1], axis, back)]
        sums = [
            landed[0].astype(f32) + part(0, block_at(-2 - step)),
            landed[1].astype(f32) + part(1, block_at(2 + step)),
        ]
        moving = sums if last else [value.astype(bf16) for value in sums]
    return moving


def ring_gather(own, axis):
    count, block_at, ahead, back = ring_place(axis)
    pieces, blocks = [own], [block_at(0)]
    down = up = own
    for step in range(1, count // 2 + 1):
        down = send(down, axis, ahead)
        pieces.append(down)
        blocks.append(block_at(-step))
        if len(pieces) < count:
            up = send(up, axis, back)
            pieces.append(up)
            blocks.append(block_at(step))
    return pieces, blocks


def after(value, done):
    return lax.optimization_barrier((value, done))[0]


def local(entry_states, down_proj, up_proj, label_rows, sampled_labels, eval_states):
    section_count = lax.axis_size("section")
    section = lax.axis_index("section")
    stage, member = section // 2, section % 2
    w_down, w_up = down_proj[0], up_proj[0]
    all_tasks, width, rank = w_down.shape
    tasks = all_tasks // 2
    micro, rows, _ = entry_states.shape
    label_count = label_rows.shape[0]
    place = jnp.stack([stage, member]).astype(jnp.int32)
    sections = range(section_count)
    swap = [(i, i ^ 1) for i in sections]
    upward = [(i, i + 2) for i in sections if i + 2 < section_count]
    downward = [(i, i - 2) for i in sections if i - 2 >= 0]

    away = (1 - member) * tasks
    down_other = send(lax.dynamic_slice_in_dim(w_down, away, tasks, 0), "section", swap)
    up_other = send(lax.dynamic_slice_in_dim(w_up, away, tasks, 0), "section", swap)
    weights = (w_down, w_up, down_other, up_other)

    held = [
        pltpu.VMEM((2, tasks, width, rank), bf16),
        pltpu.VMEM((2, tasks, width, rank), bf16),
        pltpu.SemaphoreType.DMA((2, 2, tasks)),
    ]
    params = pltpu.CompilerParams(vmem_limit_bytes=vmem_bytes)
    state_shape, hidden_shape = (tasks, rows, width), (2, tasks, rows, rank)
    wide_shape, narrow_shape = (2, 2, tasks, rows, width), (2, 2, tasks, rows, rank)
    state_type = jax.ShapeDtypeStruct(state_shape, bf16)
    square_types = (jax.ShapeDtypeStruct(wide_shape, bf16), jax.ShapeDtypeStruct(narrow_shape, bf16))
    square_scratch = [pltpu.VMEM(wide_shape, bf16), pltpu.VMEM(narrow_shape, bf16)]
    layer_flops = 4 * tasks * rows * width * rank
    weight_bytes = 8 * tasks * width * rank

    def stage_call(kernel, name, operands, outputs, scratch, copies, flops):
        return pl.pallas_call(
            kernel,
            out_shape=outputs,
            in_specs=[smem] + [hbm] * operands,
            out_specs=(hbm,) * len(outputs),
            scratch_shapes=scratch + [pltpu.SemaphoreType.DMA((copies,))] + held,
            compiler_params=params,
            cost_estimate=pl.CostEstimate(flops=flops, bytes_accessed=weight_bytes, transcendentals=0),
            name=name,
        )

    own_labels = lax.dynamic_slice_in_dim(sampled_labels, member * tasks, tasks, 0)
    label_columns = own_labels.transpose(1, 0, 2).reshape(micro, tasks * rows, 1)
    saved, crossing, returned, picked = {}, {}, {}, {}
    last_squares, first_squares = [], []
    token = place

    def at_turn(turn):
        return jnp.concatenate([token, jnp.full((1,), turn, jnp.int32)])

    def first_forward(turn):
        nonlocal token
        call = stage_call(
            first_forward_kernel, "first_forward", 5,
            (state_type, state_type, jax.ShapeDtypeStruct(hidden_shape, f32)),
            [
                pltpu.VMEM((rows, width), bf16), pltpu.VMEM(state_shape, bf16),
                pltpu.VMEM(state_shape, bf16), pltpu.VMEM(hidden_shape, f32),
            ],
            2 + 2 * tasks, 2 * layer_flops,
        )
        out, middle, hidden = call(at_turn(turn), entry_states, *weights)
        saved[turn] = (entry_states, middle, hidden)
        crossing[turn] = out
        token = after(place, hidden)

    def cross(turn):
        nonlocal token
        out = lax.optimization_barrier((crossing[turn], token))[0]
        crossing[turn] = send(out, "section", upward)

    def last_stage(turn):
        nonlocal token
        call = stage_call(
            last_stage_kernel, "last_stage", 7,
            (state_type, jax.ShapeDtypeStruct((tasks * rows, 1), f32)) + square_types,
            [
                pltpu.VMEM(state_shape, bf16), pltpu.VMEM(state_shape, bf16),
                pltpu.VMEM((tasks * rows, width), bf16), pltpu.VMEM(label_rows.shape, bf16),
                pltpu.VMEM((tasks * rows, 1), jnp.int32), pltpu.VMEM((tasks * rows, 1), f32),
                pltpu.VMEM(state_shape, bf16),
            ] + square_scratch,
            4 + 9 * tasks, 4 * layer_flops + 4 * tasks * rows * width * label_count,
        )
        grad, picked[turn], wide, narrow = call(
            at_turn(turn), crossing[turn], label_columns, label_rows, *weights
        )
        last_squares.append((wide, narrow))
        returned[turn] = send(grad, "section", downward)
        token = after(place, picked[turn])

    def first_backward(turn):
        nonlocal token
        call = stage_call(
            first_backward_kernel, "first_backward", 8, square_types,
            [
                pltpu.VMEM(state_shape, bf16), pltpu.VMEM((rows, width), bf16),
                pltpu.VMEM(state_shape, bf16), pltpu.VMEM(hidden_shape, f32),
            ] + square_scratch,
            4 + 8 * tasks, 2 * layer_flops,
        )
        squares = call(at_turn(turn), returned[turn], *saved[turn], *weights)
        first_squares.append(squares)
        token = after(place, squares[1])

    ahead, behind = min(3, micro), 2
    for turn in range(ahead):
        first_forward(turn)
        cross(turn)
    for turn in range(micro):
        if turn + ahead < micro:
            first_forward(turn + ahead)
        if turn >= behind:
            first_backward(turn - behind)
            if turn + 1 in crossing:
                token = after(token, crossing[turn + 1])
        last_stage(turn)
        if turn + ahead < micro:
            cross(turn + ahead)
    picked_all = jnp.stack([picked[turn] for turn in range(micro)], axis=0).reshape(micro, tasks, rows)
    label_logprob = jnp.zeros((micro, rows), f32)
    for index in range(tasks):
        route = [(section_count - 2 + m, m * tasks + index) for m in range(2)]
        landed = send(picked_all[:, index], "section", route)
        label_logprob = jnp.where(section % tasks == index, landed, label_logprob)

    token = after(place, label_logprob)
    for turn in range(max(micro - behind, 0), micro):
        first_backward(turn)

    block = block_size(width)

    def fisher(squares):
        turns = len(squares)
        call = pl.pallas_call(
            functools.partial(fisher_kernel, turns),
            out_shape=(jax.ShapeDtypeStruct((2, 2, width, rank), bf16),) * 2,
            grid_spec=pltpu.PrefetchScalarGridSpec(
                num_scalar_prefetch=1,
                grid=(width // block,),
                in_specs=[pl.BlockSpec((2, 2, tasks, rows, block), lambda i, s: (0, 0, 0, 0, i))] * turns
                + [pl.BlockSpec((2, 2, tasks, rows, rank), lambda i, s: (0, 0, 0, 0, 0))] * turns
                + [pl.BlockSpec((tasks, block, rank), lambda i, s: (s[1], i, 0))] * 2
                + [pl.BlockSpec((tasks, block, rank), lambda i, s: (0, i, 0))] * 2,
                out_specs=(pl.BlockSpec((2, 2, block, rank), lambda i, s: (0, 0, i, 0)),) * 2,
            ),
            compiler_params=params,
            cost_estimate=pl.CostEstimate(
                flops=8 * tasks * turns * rows * width * rank,
                bytes_accessed=turns * 8 * tasks * rows * width,
                transcendentals=0,
            ),
            name="fisher",
        )
        return call(place, *[w for w, _ in squares], *[n for _, n in squares], *weights)

    sums = lax.cond(stage == 1, lambda: fisher(last_squares), lambda: fisher(first_squares))
    other_sums = send(sums[1], "section", swap)
    shares = ring_scatter(sums[0], other_sums, "dp")
    numerator, denominator = shares
    merged_part = (numerator / (denominator + merge_eps)).astype(bf16)
    pieces, blocks = ring_gather(merged_part, "dp")
    fisher_log = jnp.log(denominator + merge_eps)

    where = jnp.stack([section] + blocks).astype(jnp.int32)
    current, result = eval_states, eval_states
    for step in range(section_count):
        result = pl.pallas_call(
            functools.partial(eval_kernel, step),
            out_shape=jax.ShapeDtypeStruct(eval_states.shape, bf16),
            in_specs=[smem] + [hbm] * (2 + len(pieces)),
            out_specs=hbm,
            scratch_shapes=[
                pltpu.VMEM(eval_states.shape, bf16), pltpu.VMEM(eval_states.shape, bf16),
                pltpu.VMEM((2, width, rank), bf16), pltpu.SemaphoreType.DMA((4 + 2 * len(pieces),)),
            ],
            compiler_params=pltpu.CompilerParams(vmem_limit_bytes=vmem_bytes),
            cost_estimate=pl.CostEstimate(
                flops=4 * eval_states.size * rank, bytes_accessed=4 * width * rank, transcendentals=0
            ),
            name="eval_block",
        )(where, current, result, *pieces)
        if step + 1 < section_count:
            current = send(result, "section", [(step, step + 1)])
    return (result[None], label_logprob[None], fisher_log[None])


def solution(mesh):
    placed = (
        P(None, "dp", None),
        P("section", None, None, None),
        P("section", None, None, None),
        P(),
        P(None, None, "dp"),
        P("dp", None),
    )
    return jax.shard_map(
        local,
        mesh=mesh,
        in_specs=placed,
        out_specs=(
            P("section", "dp", None),
            P("section", None, "dp"),
            P("section", None, "dp", None),
        ),
        check_vma=False,
    )
```

profile of v0, /device:TPU:23, one launch (start us, length us, event | category | flops | bytes accessed | tf_op | source)
XLA Modules:
  0.0 356.2 jit_solution(16922737811482273610)
XLA Ops:
  0.7 3.4 dynamic-slice_bitcast_fusion.1
  4.7 1.5 dynamic-slice_bitcast_fusion
  7.0 2.1 collective-permute-done.down_other
  9.1 3.5 collective-permute-done.1.up_other
  13.4 1.3 collective-permute-start.2
  17.1 1.3 collective-permute-start.3
  21.3 1.3 collective-permute-start.6
  23.2 10.3 %collective-permute-done.2.states = bf16[2,32,4608]{2,1,0:T(8,128)(2,1)S(1)} collective-permute-done((bf16[2,32,4608]{2,1,0:T(8,128)(2,1)}, bf16[2,32,4608]{2,1,0:T(8,128)(2,1)S(1)}, u32[]{:S(2)}, u32[]{:S(2)}) %collective-permute-start.2) | collective-permute-done | bytes 589856 | tf_op jit(solution)/shard_map/ppermute | solution.py:317
  34.3 12.6 %last_stage.5 = (bf16[2,32,4608]{2,1,0:T(8,128)(2,1)}, f32[64,1]{1,0:T(8,128)}, bf16[2,2,2,32,4608]{4,3,2,1,0:T(8,128)(2,1)}, bf16[2,2,2,32,128]{4,3,2,1,0:T(8,128)(2,1)}) custom-call(s32[3]{0:T(128)} %pad_add_fusion.1.place, bf16[2,32,4608]{2,1,0:T(8,128)(2,1)} %copy-done.18, s32[5,64,1]{2,1,0:T(8,128)} %reshape.185.labels, bf16[256,4608]{1,0:T(8,128)(2,1)} %label_rows.9, ...), custom_call_target="tpu_custom_call" | custom-call | flops 905969664 | bytes 9437184 | tf_op jit(solution)/shard_map/last_stage/pallas_call | solution.py:470
  46.9 11.8 %collective-permute-start.4 = (bf16[2,32,4608]{2,1,0:T(8,128)(2,1)}, bf16[2,32,4608]{2,1,0:T(8,128)(2,1)}, u32[]{:S(2)}, u32[]{:S(2)}) collective-permute-start(bf16[2,32,4608]{2,1,0:T(8,128)(2,1)} %get-tuple-element.210), channel_id=1, source_target_pairs={{16,0},{24,8},{17,1},{25,9},{18,2},{26,10},{19,3},{27,11},{20,4},{... | collective-permute-start | bytes 1769480 | tf_op jit(solution)/shard_map/ppermute | solution.py:317
  59.3 1.3 collective-permute-start.5
  62.8 12.3 %last_stage.6 = (bf16[2,32,4608]{2,1,0:T(8,128)(2,1)}, f32[64,1]{1,0:T(8,128)}, bf16[2,2,2,32,4608]{4,3,2,1,0:T(8,128)(2,1)}, bf16[2,2,2,32,128]{4,3,2,1,0:T(8,128)(2,1)}) custom-call(s32[3]{0:T(128)} %pad_add_fusion.4.place, bf16[2,32,4608]{2,1,0:T(8,128)(2,1)} %copy-done.17, s32[5,64,1]{2,1,0:T(8,128)} %reshape.185.labels, bf16[256,4608]{1,0:T(8,128)(2,1)} %label_rows.9, ...), custom_call_target="tpu_custom_call" | custom-call | flops 905969664 | bytes 9437184 | tf_op jit(solution)/shard_map/last_stage/pallas_call | solution.py:470
  75.1 1.3 collective-permute-start.8
  76.4 4.8 %collective-permute-start.7 = (bf16[2,32,4608]{2,1,0:T(8,128)(2,1)}, bf16[2,32,4608]{2,1,0:T(8,128)(2,1)}, u32[]{:S(2)}, u32[]{:S(2)}) collective-permute-start(bf16[2,32,4608]{2,1,0:T(8,128)(2,1)} %get-tuple-element.222), channel_id=1, source_target_pairs={{16,0},{24,8},{17,1},{25,9},{18,2},{26,10},{19,3},{27,11},{20,4},{... | collective-permute-start | bytes 1769480 | tf_op jit(solution)/shard_map/ppermute | solution.py:317
  84.9 12.5 %first_backward.5 = (bf16[2,2,2,32,4608]{4,3,2,1,0:T(8,128)(2,1)}, bf16[2,2,2,32,128]{4,3,2,1,0:T(8,128)(2,1)}) custom-call(s32[3]{0:T(128)} %pad_add_fusion.place, bf16[2,32,4608]{2,1,0:T(8,128)(2,1)} %collective-permute-done.4.grad, bf16[5,32,4608]{2,1,0:T(8,128)(2,1)} %entry.19, bf16[2,32,4608]{2,1,0:T(8,128)(2,1)} %get-tuple-element.211.middle, ...), custom_call_target="tpu_custom_call" | custom-call | flops 301989888 | bytes 9437184 | tf_op jit(solution)/shard_map/first_backward/pallas_call | solution.py:487
  98.2 12.3 %last_stage.7 = (bf16[2,32,4608]{2,1,0:T(8,128)(2,1)}, f32[64,1]{1,0:T(8,128)}, bf16[2,2,2,32,4608]{4,3,2,1,0:T(8,128)(2,1)}, bf16[2,2,2,32,128]{4,3,2,1,0:T(8,128)(2,1)}) custom-call(s32[3]{0:T(128)} %pad_add_fusion.7.place, bf16[2,32,4608]{2,1,0:T(8,128)(2,1)} %collective-permute-done.6.states, s32[5,64,1]{2,1,0:T(8,128)} %reshape.185.labels, ...), custom_call_target="tpu_custom_call" | custom-call | flops 905969664 | bytes 9437184 | tf_op jit(solution)/shard_map/last_stage/pallas_call | solution.py:470
  110.5 1.3 collective-permute-start.9
  115.9 12.5 %last_stage.8 = (bf16[2,32,4608]{2,1,0:T(8,128)(2,1)}, f32[64,1]{1,0:T(8,128)}, bf16[2,2,2,32,4608]{4,3,2,1,0:T(8,128)(2,1)}, bf16[2,2,2,32,128]{4,3,2,1,0:T(8,128)(2,1)}) custom-call(s32[3]{0:T(128)} %pad_add_fusion.10.place, bf16[2,32,4608]{2,1,0:T(8,128)(2,1)} %copy-done.13, s32[5,64,1]{2,1,0:T(8,128)} %reshape.185.labels, bf16[256,4608]{1,0:T(8,128)(2,1)} %label_rows.9, ...), custom_call_target="tpu_custom_call" | custom-call | flops 905969664 | bytes 9437184 | tf_op jit(solution)/shard_map/last_stage/pallas_call | solution.py:470
  129.4 1.3 collective-permute-start.12
  135.2 12.3 %last_stage.9 = (bf16[2,32,4608]{2,1,0:T(8,128)(2,1)}, f32[64,1]{1,0:T(8,128)}, bf16[2,2,2,32,4608]{4,3,2,1,0:T(8,128)(2,1)}, bf16[2,2,2,32,128]{4,3,2,1,0:T(8,128)(2,1)}) custom-call(s32[3]{0:T(128)} %pad_add_fusion.13.place, bf16[2,32,4608]{2,1,0:T(8,128)(2,1)} %copy-done.12, s32[5,64,1]{2,1,0:T(8,128)} %reshape.185.labels, bf16[256,4608]{1,0:T(8,128)(2,1)} %label_rows.9, ...), custom_call_target="tpu_custom_call" | custom-call | flops 905969664 | bytes 9437184 | tf_op jit(solution)/shard_map/last_stage/pallas_call | solution.py:470
  148.4 1.3 collective-permute-start.13
  151.7 4.3 %collective-permute-start.11 = (f32[5,32]{1,0:T(8,128)S(1)}, f32[5,32]{1,0:T(8,128)S(1)}, u32[]{:S(2)}, u32[]{:S(2)}) collective-permute-start(f32[5,32]{1,0:T(8,128)S(1)} %bitcast.167), channel_id=1, source_target_pairs={{16,0},{24,16},{17,1},{25,17},{18,2},{26,18},{19,3},{27,19},{20,4}... | collective-permute-start | bytes 1928 | tf_op jit(solution)/shard_map/ppermute | solution.py:317
  156.9 1.3 pad_add_fusion.9.place
  159.0 11.0 %first_backward.8 = (bf16[2,2,2,32,4608]{4,3,2,1,0:T(8,128)(2,1)}, bf16[2,2,2,32,128]{4,3,2,1,0:T(8,128)(2,1)}) custom-call(s32[3]{0:T(128)} %pad_add_fusion.9.place, bf16[2,32,4608]{2,1,0:T(8,128)(2,1)} %copy-done.14, bf16[5,32,4608]{2,1,0:T(8,128)(2,1)} %entry.19, bf16[2,32,4608]{2,1,0:T(8,128)(2,1)} %get-tuple-element.240.middle, ...), custom_call_target="tpu_custom_call" | custom-call | flops 301989888 | bytes 9437184 | tf_op jit(solution)/shard_map/first_backward/pallas_call | solution.py:487
  172.8 19.3 %conditional.1 = (bf16[2,2,4608,128]{3,2,1,0:T(8,128)(2,1)}, bf16[1,2,4608,128]{3,2,1,0:T(8,128)(2,1)}, bf16[1,2,4608,128]{3,2,1,0:T(8,128)(2,1)}) conditional(s32[]{:T(128)} %convert_element_type.224, (s32[2]{0:T(128)S(1)}, bf16[2,2,2,32,4608]{4,3,2,1,0:T(8,128)(2,1)}, bf16[2,2,2,32,4608]{4,3,2,1,0:T(8,128)(2,1)}, ...), branch_computations={%region_0.1_spmd.clone.clone, %region_1.2_spmd.clone.clone} | conditional | flops 1509949440 | bytes 21233688 | solution.py:542
  172.8 14.5 %fisher.7 = (bf16[2,2,4608,128]{3,2,1,0:T(8,128)(2,1)}, bf16[2,2,4608,128]{3,2,1,0:T(8,128)(2,1)}) custom-call(s32[2]{0:T(128)S(1)} %get-tuple-element.330.place, bf16[2,2,2,32,4608]{4,3,2,1,0:T(8,128)(2,1)} %get-tuple-element.331.refs_0_, bf16[2,2,2,32,4608]{4,3,2,1,0:T(8,128)(2,1)} %get-tuple-element.332.refs_1_, ...), custom_call_target="tpu_custom_call" | custom-call | flops 1509949440 | bytes 11796480 | tf_op jit(solution)/shard_map/cond/branch_1_fun/fisher/pallas_call | solution.py:540
  187.3 4.8 %fusion.19 = (bf16[1,2,4608,128]{3,2,1,0:T(8,128)(2,1)}, bf16[1,2,4608,128]{3,2,1,0:T(8,128)(2,1)}) fusion(bf16[2,2,4608,128]{3,2,1,0:T(8,128)(2,1)} %get-tuple-element.345), kind=kLoop, calls=%fused_computation.63 | loop fusion | bytes 9437184 | tf_op jit(solution)/shard_map/slice | solution.py:347
  192.1 6.6 %collective-permute-start.14 = (bf16[2,2,4608,128]{3,2,1,0:T(8,128)(2,1)}, bf16[2,2,4608,128]{3,2,1,0:T(8,128)(2,1)}, u32[]{:S(2)}, u32[]{:S(2)}) collective-permute-start(bf16[2,2,4608,128]{3,2,1,0:T(8,128)(2,1)} %get-tuple-element.259), channel_id=1, source_target_pairs={{0,8},{8,0},{16,24},{24,16},{1,9},{9,1},{17,25},{25,17},{2,10},{10... | collective-permute-start | bytes 14155784 | tf_op jit(solution)/shard_map/ppermute | solution.py:317
  211.9 2.7 fusion.20
  214.6 1.4 copy-done.3
  219.0 1.4 collective-permute-start.22
  221.6 4.1 %collective-permute-done.15 = bf16[2,576,128]{2,1,0:T(8,128)(2,1)S(1)} collective-permute-done((bf16[2,576,128]{2,1,0:T(8,128)(2,1)S(1)}, bf16[2,576,128]{2,1,0:T(8,128)(2,1)S(1)}, u32[]{:S(2)}, u32[]{:S(2)}) %collective-permute-start.15) | collective-permute-done | bytes 294944 | tf_op jit(solution)/shard_map/ppermute | solution.py:317
  228.5 1.4 collective-permute-start.23
  231.0 3.7 %collective-permute-done.16 = bf16[2,576,128]{2,1,0:T(8,128)(2,1)S(1)} collective-permute-done((bf16[2,576,128]{2,1,0:T(8,128)(2,1)S(1)}, bf16[2,576,128]{2,1,0:T(8,128)(2,1)S(1)}, u32[]{:S(2)}, u32[]{:S(2)}) %collective-permute-start.16) | collective-permute-done | bytes 294944 | tf_op jit(solution)/shard_map/ppermute | solution.py:317
  234.7 1.2 fusion.13
  237.2 1.4 collective-permute-start.24
  239.9 2.9 collective-permute-done.17
  245.3 1.4 collective-permute-start.25
  248.0 2.0 collective-permute-done.18
  252.5 1.4 collective-permute-start.26
  255.2 1.6 collective-permute-done.19
  259.5 1.4 collective-permute-start.27
  262.1 1.9 collective-permute-done.20
  264.0 1.3 fusion.9
  265.5 1.8 fusion.1
  267.3 1.3 collective-permute-start.28
  269.9 2.2 collective-permute-done.21
  272.1 1.6 collective-permute-done.28
  273.7 2.3 log_bitcast_fusion
  276.2 1.3 collective-permute-start.30
  277.5 4.4 %collective-permute-done.29.refs_1_ = bf16[2,576,128]{2,1,0:T(8,128)(2,1)S(1)} collective-permute-done((bf16[2,576,128]{2,1,0:T(8,128)(2,1)S(1)}, bf16[2,576,128]{2,1,0:T(8,128)(2,1)S(1)}, u32[]{:S(2)}, u32[]{:S(2)}) %collective-permute-start.29) | collective-permute-done | bytes 294944 | tf_op jit(solution)/shard_map/ppermute | solution.py:317
  282.1 1.8 collective-permute-done.30.refs_2_
  283.9 1.3 collective-permute-start.32
  285.2 2.3 collective-permute-done.31.refs_3_
  287.7 2.7 collective-permute-done.32.refs_4_
  291.3 3.7 %collective-permute-done.33.refs_5_ = bf16[2,576,128]{2,1,0:T(8,128)(2,1)S(1)} collective-permute-done((bf16[2,576,128]{2,1,0:T(8,128)(2,1)S(1)}, bf16[2,576,128]{2,1,0:T(8,128)(2,1)S(1)}, u32[]{:S(2)}, u32[]{:S(2)}) %collective-permute-start.33) | collective-permute-done | bytes 294944 | tf_op jit(solution)/shard_map/ppermute | solution.py:317
  295.1 5.6 %stack.34.where = s32[9]{0:T(128)} concatenate(s32[1]{0:T(128)} %bitcast, s32[1]{0:T(128)} %get-tuple-element.375, s32[1]{0:T(128)} %get-tuple-element.374, s32[1]{0:T(128)} %get-tuple-element.373, s32[1]{0:T(128)} %get-tuple-element.372, s32[1]{0:T(128)} %get-tuple-element.371, s32[1]{0:T(128)} %get-tuple-element.370, s32[1]{0:T(128)} %get-tuple-element.369, s32[1]{0:T(128)} %get-tuple-element.368), dimensions={0} | concatenate | bytes 72 | tf_op jit(solution)/shard_map/stack | solution.py:550
  300.7 3.3 collective-permute-done.35.refs_7_
  304.8 2.5 eval_block.4.before
  308.7 2.5 eval_block.5.before
  312.6 2.6 eval_block.6.before
  315.3 1.3 collective-permute-start.38
  317.2 34.3 %collective-permute-done.38.states = bf16[32,4608]{1,0:T(8,128)(2,1)S(1)} collective-permute-done((bf16[32,4608]{1,0:T(8,128)(2,1)}, bf16[32,4608]{1,0:T(8,128)(2,1)S(1)}, u32[]{:S(2)}, u32[]{:S(2)}) %collective-permute-start.38) | collective-permute-done | bytes 294944 | tf_op jit(solution)/shard_map/ppermute | solution.py:317
  352.2 3.8 %eval_block.7 = bf16[32,4608]{1,0:T(8,128)(2,1)} custom-call(s32[9]{0:T(128)} %stack.34.where, bf16[32,4608]{1,0:T(8,128)(2,1)} %copy-done.19, bf16[32,4608]{1,0:T(8,128)(2,1)} %eval_block.6.before, bf16[2,576,128]{2,1,0:T(8,128)(2,1)} %copy-done.4, bf16[2,576,128]{2,1,0:T(8,128)(2,1)} %copy-done.5, bf16[2,576,128]{2,1,0:T(8,128)(2,1)} %copy-done.6, ...), custom_call_target="tpu_custom_call" | custom-call | flops 75497472 | bytes 2359296 | tf_op jit(solution)/shard_map/eval_block/pallas_call | solution.py:553
  (190 shorter events, 54.9 us)
Async XLA Ops:
  0.6 14.1 %copy-start = (s32[4,5,32]{2,0,1:T(4,128)S(1)}, s32[4,5,32]{2,0,1:T(4,128)}, u32[]{:S(2)}) copy-start(s32[4,5,32]{2,0,1:T(4,128)} %param.16) | copy-start | bytes 7684
  0.7 4.0 %copy-start.2 = (bf16[1,4,4608,128]{3,2,1,0:T(8,128)(2,1)S(1)}, bf16[1,4,4608,128]{3,2,1,0:T(8,128)(2,1)}, u32[]{:S(2)}) copy-start(bf16[1,4,4608,128]{3,2,1,0:T(8,128)(2,1)} %param.14) | copy-start | bytes 14155780
  4.0 5.0 %collective-permute-start = (bf16[2,4608,128]{2,1,0:T(8,128)(2,1)}, bf16[2,4608,128]{2,1,0:T(8,128)(2,1)S(1)}, u32[]{:S(2)}, u32[]{:S(2)}) collective-permute-start(bf16[2,4608,128]{2,1,0:T(8,128)(2,1)} %dynamic-slice_bitcast_fusion.1), channel_id=1, source_target_pairs={{0,8},{8,0},{16,24},{24,16},{1,9},{9,1},{17,25},{25,17},{2,10},{10... | collective-permute-start | bytes 7077896 | tf_op jit(solution)/shard_map/ppermute | solution.py:317
  6.3 6.3 %collective-permute-start.1 = (bf16[2,4608,128]{2,1,0:T(8,128)(2,1)}, bf16[2,4608,128]{2,1,0:T(8,128)(2,1)}, u32[]{:S(2)}, u32[]{:S(2)}) collective-permute-start(bf16[2,4608,128]{2,1,0:T(8,128)(2,1)} %dynamic-slice_bitcast_fusion), channel_id=1, source_target_pairs={{0,8},{8,0},{16,24},{24,16},{1,9},{9,1},{17,25},{25,17},{2,10},{10... | collective-permute-start | bytes 7077896 | tf_op jit(solution)/shard_map/ppermute | solution.py:317
  6.3 128.0 %copy-start.32 = (s32[2]{0:T(128)}, s32[2]{0:T(128)S(1)}, u32[]{:S(2)}) copy-start(s32[2]{0:T(128)S(1)} %pad_add_fusion.15) | copy-start | bytes 28
  13.4 20.1 %collective-permute-start.2 = (bf16[2,32,4608]{2,1,0:T(8,128)(2,1)}, bf16[2,32,4608]{2,1,0:T(8,128)(2,1)S(1)}, u32[]{:S(2)}, u32[]{:S(2)}) collective-permute-start(bf16[2,32,4608]{2,1,0:T(8,128)(2,1)} %get-tuple-element.201), channel_id=1, source_target_pairs={{0,16},{8,24},{1,17},{9,25},{2,18},{10,26},{3,19},{11,27},{4,20},{... | collective-permute-start | bytes 1769480 | tf_op jit(solution)/shard_map/ppermute | solution.py:317
  15.6 3.5 slice-start
  16.2 2.9 slice-start.1
  17.1 44.9 %collective-permute-start.3 = (bf16[2,32,4608]{2,1,0:T(8,128)(2,1)}, bf16[2,32,4608]{2,1,0:T(8,128)(2,1)S(1)}, u32[]{:S(2)}, u32[]{:S(2)}) collective-permute-start(bf16[2,32,4608]{2,1,0:T(8,128)(2,1)} %get-tuple-element.207), channel_id=1, source_target_pairs={{0,16},{8,24},{1,17},{9,25},{2,18},{10,26},{3,19},{11,27},{4,20},{... | collective-permute-start | bytes 1769480 | tf_op jit(solution)/shard_map/ppermute | solution.py:317
  21.3 76.9 %collective-permute-start.6 = (bf16[2,32,4608]{2,1,0:T(8,128)(2,1)}, bf16[2,32,4608]{2,1,0:T(8,128)(2,1)}, u32[]{:S(2)}, u32[]{:S(2)}) collective-permute-start(bf16[2,32,4608]{2,1,0:T(8,128)(2,1)} %get-tuple-element.219), channel_id=1, source_target_pairs={{0,16},{8,24},{1,17},{9,25},{2,18},{10,26},{3,19},{11,27},{4,20},{... | collective-permute-start | bytes 1769480 | tf_op jit(solution)/shard_map/ppermute | solution.py:317
  46.9 38.1 %collective-permute-start.4 = (bf16[2,32,4608]{2,1,0:T(8,128)(2,1)}, bf16[2,32,4608]{2,1,0:T(8,128)(2,1)}, u32[]{:S(2)}, u32[]{:S(2)}) collective-permute-start(bf16[2,32,4608]{2,1,0:T(8,128)(2,1)} %get-tuple-element.210), channel_id=1, source_target_pairs={{16,0},{24,8},{17,1},{25,9},{18,2},{26,10},{19,3},{27,11},{20,4},{... | collective-permute-start | bytes 1769480 | tf_op jit(solution)/shard_map/ppermute | solution.py:317
  59.3 38.1 %collective-permute-start.5 = (bf16[2,32,4608]{2,1,0:T(8,128)(2,1)}, bf16[2,32,4608]{2,1,0:T(8,128)(2,1)S(1)}, u32[]{:S(2)}, u32[]{:S(2)}) collective-permute-start(bf16[2,32,4608]{2,1,0:T(8,128)(2,1)} %get-tuple-element.216), channel_id=1, source_target_pairs={{0,16},{8,24},{1,17},{9,25},{2,18},{10,26},{3,19},{11,27},{4,20},{... | collective-permute-start | bytes 1769480 | tf_op jit(solution)/shard_map/ppermute | solution.py:317
  75.1 39.4 %collective-permute-start.8 = (bf16[2,32,4608]{2,1,0:T(8,128)(2,1)}, bf16[2,32,4608]{2,1,0:T(8,128)(2,1)S(1)}, u32[]{:S(2)}, u32[]{:S(2)}) collective-permute-start(bf16[2,32,4608]{2,1,0:T(8,128)(2,1)} %get-tuple-element.228), channel_id=1, source_target_pairs={{0,16},{8,24},{1,17},{9,25},{2,18},{10,26},{3,19},{11,27},{4,20},{... | collective-permute-start | bytes 1769480 | tf_op jit(solution)/shard_map/ppermute | solution.py:317
  76.4 37.0 %collective-permute-start.7 = (bf16[2,32,4608]{2,1,0:T(8,128)(2,1)}, bf16[2,32,4608]{2,1,0:T(8,128)(2,1)}, u32[]{:S(2)}, u32[]{:S(2)}) collective-permute-start(bf16[2,32,4608]{2,1,0:T(8,128)(2,1)} %get-tuple-element.222), channel_id=1, source_target_pairs={{16,0},{24,8},{17,1},{25,9},{18,2},{26,10},{19,3},{27,11},{20,4},{... | collective-permute-start | bytes 1769480 | tf_op jit(solution)/shard_map/ppermute | solution.py:317
  84.9 13.3 %slice-start.2 = ((s8[4718592]{0:T(1024)(128)(4,1)}), s8[4194304]{0:T(1024)(128)(4,1)S(1)}, s32[]{:S(2)}) async-start(s8[4718592]{0:T(1024)(128)(4,1)} %bitcast.133), calls=%async_computation.2 | async-start | bytes 8388608
  84.9 13.3 %slice-start.3 = ((s8[4718592]{0:T(1024)(128)(4,1)}), s8[524288]{0:T(1024)(128)(4,1)S(1)}, s32[]{:S(2)}) async-start(s8[4718592]{0:T(1024)(128)(4,1)} %bitcast.133), calls=%async_computation.3 | async-start | bytes 1048576
  97.4 13.1 %copy-start.13 = (bf16[2,32,4608]{2,1,0:T(8,128)(2,1)}, bf16[2,32,4608]{2,1,0:T(8,128)(2,1)S(1)}, u32[]{:S(2)}) copy-start(bf16[2,32,4608]{2,1,0:T(8,128)(2,1)S(1)} %collective-permute-done.5.states) | copy-start | bytes 1769476
  110.5 22.0 %collective-permute-start.9 = (bf16[2,32,4608]{2,1,0:T(8,128)(2,1)}, bf16[2,32,4608]{2,1,0:T(8,128)(2,1)S(1)}, u32[]{:S(2)}, u32[]{:S(2)}) collective-permute-start(bf16[2,32,4608]{2,1,0:T(8,128)(2,1)} %get-tuple-element.232), channel_id=1, source_target_pairs={{16,0},{24,8},{17,1},{25,9},{18,2},{26,10},{19,3},{27,11},{20,4},{... | collective-permute-start | bytes 1769480 | tf_op jit(solution)/shard_map/ppermute | solution.py:317
  113.4 2.4 slice-start.4
  113.4 2.5 slice-start.5
  114.5 13.9 %copy-start.12 = (bf16[2,32,4608]{2,1,0:T(8,128)(2,1)}, bf16[2,32,4608]{2,1,0:T(8,128)(2,1)S(1)}, u32[]{:S(2)}) copy-start(bf16[2,32,4608]{2,1,0:T(8,128)(2,1)S(1)} %collective-permute-done.8.states) | copy-start | bytes 1769476
  129.4 28.8 %collective-permute-start.12 = (bf16[2,32,4608]{2,1,0:T(8,128)(2,1)}, bf16[2,32,4608]{2,1,0:T(8,128)(2,1)S(1)}, u32[]{:S(2)}, u32[]{:S(2)}) collective-permute-start(bf16[2,32,4608]{2,1,0:T(8,128)(2,1)} %get-tuple-element.239), channel_id=1, source_target_pairs={{16,0},{24,8},{17,1},{25,9},{18,2},{26,10},{19,3},{27,11},{20,4},{... | collective-permute-start | bytes 1769480 | tf_op jit(solution)/shard_map/ppermute | solution.py:317
  132.5 2.6 slice-start.6
  148.4 22.3 %collective-permute-start.13 = (bf16[2,32,4608]{2,1,0:T(8,128)(2,1)}, bf16[2,32,4608]{2,1,0:T(8,128)(2,1)S(1)}, u32[]{:S(2)}, u32[]{:S(2)}) collective-permute-start(bf16[2,32,4608]{2,1,0:T(8,128)(2,1)} %get-tuple-element.244), channel_id=1, source_target_pairs={{16,0},{24,8},{17,1},{25,9},{18,2},{26,10},{19,3},{27,11},{20,4},{... | collective-permute-start | bytes 1769480 | tf_op jit(solution)/shard_map/ppermute | solution.py:317
  151.1 5.0 %collective-permute-start.10 = (f32[5,32]{1,0:T(8,128)S(1)}, f32[5,32]{1,0:T(8,128)S(1)}, u32[]{:S(2)}, u32[]{:S(2)}) collective-permute-start(f32[5,32]{1,0:T(8,128)S(1)} %bitcast.166), channel_id=1, source_target_pairs={{16,8},{24,24},{17,9},{25,25},{18,10},{26,26},{19,11},{27,27},{20,... | collective-permute-start | bytes 1928 | tf_op jit(solution)/shard_map/ppermute | solution.py:317
  151.7 5.1 %collective-permute-start.11 = (f32[5,32]{1,0:T(8,128)S(1)}, f32[5,32]{1,0:T(8,128)S(1)}, u32[]{:S(2)}, u32[]{:S(2)}) collective-permute-start(f32[5,32]{1,0:T(8,128)S(1)} %bitcast.167), channel_id=1, source_target_pairs={{16,0},{24,16},{17,1},{25,17},{18,2},{26,18},{19,3},{27,19},{20,4}... | collective-permute-start | bytes 1928 | tf_op jit(solution)/shard_map/ppermute | solution.py:317
  158.2 13.3 %slice-start.8 = ((s8[4718592]{0:T(1024)(128)(4,1)}), s8[4194304]{0:T(1024)(128)(4,1)S(1)}, s32[]{:S(2)}) async-start(s8[4718592]{0:T(1024)(128)(4,1)} %bitcast.142), calls=%async_computation.8 | async-start | bytes 8388608
  159.0 11.0 %copy-start.33 = (s32[2]{0:T(128)S(1)}, s32[2]{0:T(128)}, u32[]{:S(2)}) copy-start(s32[2]{0:T(128)} %copy-done.32) | copy-start | bytes 28
  159.0 12.5 %slice-start.9 = ((s8[4718592]{0:T(1024)(128)(4,1)}), s8[524288]{0:T(1024)(128)(4,1)S(1)}, s32[]{:S(2)}) async-start(s8[4718592]{0:T(1024)(128)(4,1)} %bitcast.142), calls=%async_computation.9 | async-start | bytes 1048576
  172.7 26.0 %copy-start.34 = (s32[8]{0:T(128)S(1)}, s32[8]{0:T(128)}, u32[]{:S(2)}) copy-start(s32[8]{0:T(128)} %constant.240.clone) | copy-start | bytes 100
  172.8 37.7 %copy-start.22 = (s32[8]{0:T(128)S(1)}, s32[8]{0:T(128)}, u32[]{:S(2)}) copy-start(s32[8]{0:T(128)} %constant.241.clone) | copy-start | bytes 100
  192.1 19.8 %collective-permute-start.14 = (bf16[2,2,4608,128]{3,2,1,0:T(8,128)(2,1)}, bf16[2,2,4608,128]{3,2,1,0:T(8,128)(2,1)}, u32[]{:S(2)}, u32[]{:S(2)}) collective-permute-start(bf16[2,2,4608,128]{3,2,1,0:T(8,128)(2,1)} %get-tuple-element.259), channel_id=1, source_target_pairs={{0,8},{8,0},{16,24},{24,16},{1,9},{9,1},{17,25},{25,17},{2,10},{10... | collective-permute-start | bytes 14155784 | tf_op jit(solution)/shard_map/ppermute | solution.py:317
  217.0 8.7 %collective-permute-start.15 = (bf16[2,576,128]{2,1,0:T(8,128)(2,1)S(1)}, bf16[2,576,128]{2,1,0:T(8,128)(2,1)S(1)}, u32[]{:S(2)}, u32[]{:S(2)}) collective-permute-start(bf16[2,576,128]{2,1,0:T(8,128)(2,1)S(1)} %fusion.15), channel_id=1, source_target_pairs={{0,2},{2,4},{4,6},{6,7},{7,5},{5,3},{3,1},{1,0},{8,10},{10,12},{12... | collective-permute-start | bytes 884744 | tf_op jit(solution)/shard_map/ppermute | solution.py:317
  219.0 8.4 %collective-permute-start.22 = (bf16[2,576,128]{2,1,0:T(8,128)(2,1)S(1)}, bf16[2,576,128]{2,1,0:T(8,128)(2,1)S(1)}, u32[]{:S(2)}, u32[]{:S(2)}) collective-permute-start(bf16[2,576,128]{2,1,0:T(8,128)(2,1)S(1)} %fusion.16), channel_id=1, source_target_pairs={{2,0},{4,2},{6,4},{7,6},{5,7},{3,5},{1,3},{0,1},{10,8},{12,10},{14... | collective-permute-start | bytes 884744 | tf_op jit(solution)/shard_map/ppermute | solution.py:317
  226.9 7.8 %collective-permute-start.16 = (bf16[2,576,128]{2,1,0:T(8,128)(2,1)S(1)}, bf16[2,576,128]{2,1,0:T(8,128)(2,1)S(1)}, u32[]{:S(2)}, u32[]{:S(2)}) collective-permute-start(bf16[2,576,128]{2,1,0:T(8,128)(2,1)S(1)} %fusion.14), channel_id=1, source_target_pairs={{0,2},{2,4},{4,6},{6,7},{7,5},{5,3},{3,1},{1,0},{8,10},{10,12},{12... | collective-permute-start | bytes 884744 | tf_op jit(solution)/shard_map/ppermute | solution.py:317
  228.5 7.7 %collective-permute-start.23 = (bf16[2,576,128]{2,1,0:T(8,128)(2,1)S(1)}, bf16[2,576,128]{2,1,0:T(8,128)(2,1)S(1)}, u32[]{:S(2)}, u32[]{:S(2)}) collective-permute-start(bf16[2,576,128]{2,1,0:T(8,128)(2,1)S(1)} %fusion.6), channel_id=1, source_target_pairs={{2,0},{4,2},{6,4},{7,6},{5,7},{3,5},{1,3},{0,1},{10,8},{12,10},{14... | collective-permute-start | bytes 884744 | tf_op jit(solution)/shard_map/ppermute | solution.py:317
  235.9 6.9 %collective-permute-start.17 = (bf16[2,576,128]{2,1,0:T(8,128)(2,1)S(1)}, bf16[2,576,128]{2,1,0:T(8,128)(2,1)S(1)}, u32[]{:S(2)}, u32[]{:S(2)}) collective-permute-start(bf16[2,576,128]{2,1,0:T(8,128)(2,1)S(1)} %fusion.13), channel_id=1, source_target_pairs={{0,2},{2,4},{4,6},{6,7},{7,5},{5,3},{3,1},{1,0},{8,10},{10,12},{12... | collective-permute-start | bytes 884744 | tf_op jit(solution)/shard_map/ppermute | solution.py:317
  237.2 7.0 %collective-permute-start.24 = (bf16[2,576,128]{2,1,0:T(8,128)(2,1)S(1)}, bf16[2,576,128]{2,1,0:T(8,128)(2,1)S(1)}, u32[]{:S(2)}, u32[]{:S(2)}) collective-permute-start(bf16[2,576,128]{2,1,0:T(8,128)(2,1)S(1)} %fusion.5), channel_id=1, source_target_pairs={{2,0},{4,2},{6,4},{7,6},{5,7},{3,5},{1,3},{0,1},{10,8},{12,10},{14... | collective-permute-start | bytes 884744 | tf_op jit(solution)/shard_map/ppermute | solution.py:317
  244.0 6.0 %collective-permute-start.18 = (bf16[2,576,128]{2,1,0:T(8,128)(2,1)S(1)}, bf16[2,576,128]{2,1,0:T(8,128)(2,1)S(1)}, u32[]{:S(2)}, u32[]{:S(2)}) collective-permute-start(bf16[2,576,128]{2,1,0:T(8,128)(2,1)S(1)} %fusion.12), channel_id=1, source_target_pairs={{0,2},{2,4},{4,6},{6,7},{7,5},{5,3},{3,1},{1,0},{8,10},{10,12},{12... | collective-permute-start | bytes 884744 | tf_op jit(solution)/shard_map/ppermute | solution.py:317
  245.3 6.0 %collective-permute-start.25 = (bf16[2,576,128]{2,1,0:T(8,128)(2,1)S(1)}, bf16[2,576,128]{2,1,0:T(8,128)(2,1)S(1)}, u32[]{:S(2)}, u32[]{:S(2)}) collective-permute-start(bf16[2,576,128]{2,1,0:T(8,128)(2,1)S(1)} %fusion.4), channel_id=1, source_target_pairs={{2,0},{4,2},{6,4},{7,6},{5,7},{3,5},{1,3},{0,1},{10,8},{12,10},{14... | collective-permute-start | bytes 884744 | tf_op jit(solution)/shard_map/ppermute | solution.py:317
  251.1 5.6 %collective-permute-start.19 = (bf16[2,576,128]{2,1,0:T(8,128)(2,1)S(1)}, bf16[2,576,128]{2,1,0:T(8,128)(2,1)S(1)}, u32[]{:S(2)}, u32[]{:S(2)}) collective-permute-start(bf16[2,576,128]{2,1,0:T(8,128)(2,1)S(1)} %fusion.11), channel_id=1, source_target_pairs={{0,2},{2,4},{4,6},{6,7},{7,5},{5,3},{3,1},{1,0},{8,10},{10,12},{12... | collective-permute-start | bytes 884744 | tf_op jit(solution)/shard_map/ppermute | solution.py:317
  252.5 5.9 %collective-permute-start.26 = (bf16[2,576,128]{2,1,0:T(8,128)(2,1)S(1)}, bf16[2,576,128]{2,1,0:T(8,128)(2,1)S(1)}, u32[]{:S(2)}, u32[]{:S(2)}) collective-permute-start(bf16[2,576,128]{2,1,0:T(8,128)(2,1)S(1)} %fusion.3), channel_id=1, source_target_pairs={{2,0},{4,2},{6,4},{7,6},{5,7},{3,5},{1,3},{0,1},{10,8},{12,10},{14... | collective-permute-start | bytes 884744 | tf_op jit(solution)/shard_map/ppermute | solution.py:317
  258.0 6.0 %collective-permute-start.20 = (bf16[2,576,128]{2,1,0:T(8,128)(2,1)S(1)}, bf16[2,576,128]{2,1,0:T(8,128)(2,1)}, u32[]{:S(2)}, u32[]{:S(2)}) collective-permute-start(bf16[2,576,128]{2,1,0:T(8,128)(2,1)S(1)} %fusion.10), channel_id=1, source_target_pairs={{0,2},{2,4},{4,6},{6,7},{7,5},{5,3},{3,1},{1,0},{8,10},{10,12},{12... | collective-permute-start | bytes 884744 | tf_op jit(solution)/shard_map/ppermute | solution.py:317
  259.5 6.0 %collective-permute-start.27 = (bf16[2,576,128]{2,1,0:T(8,128)(2,1)S(1)}, bf16[2,576,128]{2,1,0:T(8,128)(2,1)S(1)}, u32[]{:S(2)}, u32[]{:S(2)}) collective-permute-start(bf16[2,576,128]{2,1,0:T(8,128)(2,1)S(1)} %fusion.2), channel_id=1, source_target_pairs={{2,0},{4,2},{6,4},{7,6},{5,7},{3,5},{1,3},{0,1},{10,8},{12,10},{14... | collective-permute-start | bytes 884744 | tf_op jit(solution)/shard_map/ppermute | solution.py:317
  265.3 6.9 %collective-permute-start.21 = (bf16[2,576,128]{2,1,0:T(8,128)(2,1)S(1)}, bf16[2,576,128]{2,1,0:T(8,128)(2,1)S(1)}, u32[]{:S(2)}, u32[]{:S(2)}) collective-permute-start(bf16[2,576,128]{2,1,0:T(8,128)(2,1)S(1)} %fusion.9), channel_id=1, source_target_pairs={{0,2},{2,4},{4,6},{6,7},{7,5},{5,3},{3,1},{1,0},{8,10},{10,12},{12... | collective-permute-start | bytes 884744 | tf_op jit(solution)/shard_map/ppermute | solution.py:317
  267.3 6.4 %collective-permute-start.28 = (bf16[2,576,128]{2,1,0:T(8,128)(2,1)}, bf16[2,576,128]{2,1,0:T(8,128)(2,1)S(1)}, u32[]{:S(2)}, u32[]{:S(2)}) collective-permute-start(bf16[2,576,128]{2,1,0:T(8,128)(2,1)} %fusion.1), channel_id=1, source_target_pairs={{2,0},{4,2},{6,4},{7,6},{5,7},{3,5},{1,3},{0,1},{10,8},{12,10},{14... | collective-permute-start | bytes 884744 | tf_op jit(solution)/shard_map/ppermute | solution.py:317
  276.0 28.0 %copy-start.4 = (bf16[2,576,128]{2,1,0:T(8,128)(2,1)}, bf16[2,576,128]{2,1,0:T(8,128)(2,1)S(1)}, u32[]{:S(2)}) copy-start(bf16[2,576,128]{2,1,0:T(8,128)(2,1)S(1)} %get-tuple-element.355.refs_0_) | copy-start | bytes 884740
  276.0 5.9 %collective-permute-start.29 = (bf16[2,576,128]{2,1,0:T(8,128)(2,1)S(1)}, bf16[2,576,128]{2,1,0:T(8,128)(2,1)S(1)}, u32[]{:S(2)}, u32[]{:S(2)}) collective-permute-start(bf16[2,576,128]{2,1,0:T(8,128)(2,1)S(1)} %get-tuple-element.355.refs_0_), channel_id=1, source_target_pairs={{0,2},{2,4},{4,6},{6,7},{7,5},{5,3},{3,1},{1,0},{8,10},{10,12},{12... | collective-permute-start | bytes 884744 | tf_op jit(solution)/shard_map/ppermute | solution.py:317
  276.2 7.7 %collective-permute-start.30 = (bf16[2,576,128]{2,1,0:T(8,128)(2,1)S(1)}, bf16[2,576,128]{2,1,0:T(8,128)(2,1)S(1)}, u32[]{:S(2)}, u32[]{:S(2)}) collective-permute-start(bf16[2,576,128]{2,1,0:T(8,128)(2,1)S(1)} %get-tuple-element.355.refs_0_), channel_id=1, source_target_pairs={{2,0},{4,2},{6,4},{7,6},{5,7},{3,5},{1,3},{0,1},{10,8},{12,10},{14... | collective-permute-start | bytes 884744 | tf_op jit(solution)/shard_map/ppermute | solution.py:317
  281.9 22.1 %copy-start.5 = (bf16[2,576,128]{2,1,0:T(8,128)(2,1)}, bf16[2,576,128]{2,1,0:T(8,128)(2,1)S(1)}, u32[]{:S(2)}) copy-start(bf16[2,576,128]{2,1,0:T(8,128)(2,1)S(1)} %collective-permute-done.29.refs_1_) | copy-start | bytes 884740
  281.9 5.6 %collective-permute-start.31 = (bf16[2,576,128]{2,1,0:T(8,128)(2,1)S(1)}, bf16[2,576,128]{2,1,0:T(8,128)(2,1)S(1)}, u32[]{:S(2)}, u32[]{:S(2)}) collective-permute-start(bf16[2,576,128]{2,1,0:T(8,128)(2,1)S(1)} %collective-permute-done.29.refs_1_), channel_id=1, source_target_pairs={{0,2},{2,4},{4,6},{6,7},{7,5},{5,3},{3,1},{1,0},{8,10},{10,12},{12... | collective-permute-start | bytes 884744 | tf_op jit(solution)/shard_map/ppermute | solution.py:317
  283.9 20.1 %copy-start.6 = (bf16[2,576,128]{2,1,0:T(8,128)(2,1)}, bf16[2,576,128]{2,1,0:T(8,128)(2,1)S(1)}, u32[]{:S(2)}) copy-start(bf16[2,576,128]{2,1,0:T(8,128)(2,1)S(1)} %collective-permute-done.30.refs_2_) | copy-start | bytes 884740
  283.9 6.4 %collective-permute-start.32 = (bf16[2,576,128]{2,1,0:T(8,128)(2,1)S(1)}, bf16[2,576,128]{2,1,0:T(8,128)(2,1)S(1)}, u32[]{:S(2)}, u32[]{:S(2)}) collective-permute-start(bf16[2,576,128]{2,1,0:T(8,128)(2,1)S(1)} %collective-permute-done.30.refs_2_), channel_id=1, source_target_pairs={{2,0},{4,2},{6,4},{7,6},{5,7},{3,5},{1,3},{0,1},{10,8},{12,10},{14... | collective-permute-start | bytes 884744 | tf_op jit(solution)/shard_map/ppermute | solution.py:317
  287.5 16.5 %copy-start.7 = (bf16[2,576,128]{2,1,0:T(8,128)(2,1)}, bf16[2,576,128]{2,1,0:T(8,128)(2,1)S(1)}, u32[]{:S(2)}) copy-start(bf16[2,576,128]{2,1,0:T(8,128)(2,1)S(1)} %collective-permute-done.31.refs_3_) | copy-start | bytes 884740
  287.5 7.6 %collective-permute-start.33 = (bf16[2,576,128]{2,1,0:T(8,128)(2,1)S(1)}, bf16[2,576,128]{2,1,0:T(8,128)(2,1)S(1)}, u32[]{:S(2)}, u32[]{:S(2)}) collective-permute-start(bf16[2,576,128]{2,1,0:T(8,128)(2,1)S(1)} %collective-permute-done.31.refs_3_), channel_id=1, source_target_pairs={{0,2},{2,4},{4,6},{6,7},{7,5},{5,3},{3,1},{1,0},{8,10},{10,12},{12... | collective-permute-start | bytes 884744 | tf_op jit(solution)/shard_map/ppermute | solution.py:317
  290.3 13.7 %copy-start.8 = (bf16[2,576,128]{2,1,0:T(8,128)(2,1)}, bf16[2,576,128]{2,1,0:T(8,128)(2,1)S(1)}, u32[]{:S(2)}) copy-start(bf16[2,576,128]{2,1,0:T(8,128)(2,1)S(1)} %collective-permute-done.32.refs_4_) | copy-start | bytes 884740
  290.3 10.3 %collective-permute-start.34 = (bf16[2,576,128]{2,1,0:T(8,128)(2,1)S(1)}, bf16[2,576,128]{2,1,0:T(8,128)(2,1)S(1)}, u32[]{:S(2)}, u32[]{:S(2)}) collective-permute-start(bf16[2,576,128]{2,1,0:T(8,128)(2,1)S(1)} %collective-permute-done.32.refs_4_), channel_id=1, source_target_pairs={{2,0},{4,2},{6,4},{7,6},{5,7},{3,5},{1,3},{0,1},{10,8},{12,10},{14... | collective-permute-start | bytes 884744 | tf_op jit(solution)/shard_map/ppermute | solution.py:317
  295.0 9.0 %copy-start.9 = (bf16[2,576,128]{2,1,0:T(8,128)(2,1)}, bf16[2,576,128]{2,1,0:T(8,128)(2,1)S(1)}, u32[]{:S(2)}) copy-start(bf16[2,576,128]{2,1,0:T(8,128)(2,1)S(1)} %collective-permute-done.33.refs_5_) | copy-start | bytes 884740
  295.0 8.9 %collective-permute-start.35 = (bf16[2,576,128]{2,1,0:T(8,128)(2,1)S(1)}, bf16[2,576,128]{2,1,0:T(8,128)(2,1)S(1)}, u32[]{:S(2)}, u32[]{:S(2)}) collective-permute-start(bf16[2,576,128]{2,1,0:T(8,128)(2,1)S(1)} %collective-permute-done.33.refs_5_), channel_id=1, source_target_pairs={{0,2},{2,4},{4,6},{6,7},{7,5},{5,3},{3,1},{1,0},{8,10},{10,12},{12... | collective-permute-start | bytes 884744 | tf_op jit(solution)/shard_map/ppermute | solution.py:317
  300.7 3.4 copy-start.10
  307.3 0.7 collective-permute-start.36
  311.2 0.7 collective-permute-start.37
  312.6 43.4 %copy-start.1 = (s32[4,5,32]{2,0,1:T(4,128)S(1)}, s32[4,5,32]{2,0,1:T(4,128)}, u32[]{:S(2)}) copy-start(s32[4,5,32]{2,0,1:T(4,128)} %param.16) | copy-start | bytes 7684
  315.3 36.2 %collective-permute-start.38 = (bf16[32,4608]{1,0:T(8,128)(2,1)}, bf16[32,4608]{1,0:T(8,128)(2,1)S(1)}, u32[]{:S(2)}, u32[]{:S(2)}) collective-permute-start(bf16[32,4608]{1,0:T(8,128)(2,1)} %eval_block.6.before), channel_id=1, source_target_pairs={{16,24},{17,25},{18,26},{19,27},{20,28},{21,29},{22,30},{23,31}} | collective-permute-start | bytes 884744 | tf_op jit(solution)/shard_map/ppermute | solution.py:317
  (20 other events, 20.6 us)
where the time goes:
time: 362 us; the launch traced here: 356 us
  Pallas kernels  119 us (33%)
  waiting for transfers between devices  89.7 us (25%)
  starting transfers between devices  57.1 us (16%)
  local copies, waits for them, and re-layouts  34.1 us (9%)
  other arithmetic  33.7 us (9%)
  between operations  23 us (6%)
    ppermute x39, waiting for transfers between devices, send(): return lax.ppermute(block, axis, route)  89.7 us
    pallas_call x5, Pallas kernels, last_stage(): call(at_turn(turn), crossing[turn], label_columns, label_rows, *weights)  61.9 us
    ppermute x39, starting transfers between devices, send(): return lax.ppermute(block, axis, route)  57.1 us
    pallas_call x5, Pallas kernels, first_backward(): squares = call(at_turn(turn), returned[turn], *saved[turn], *weights)  26.6 us
    convert_element_type x12, other arithmetic, ring_scatter(): moving = sums if last else [value.astype(bf16) for value in sums]  14.6 us
    pallas_call x1, Pallas kernels, fisher(): call(place, *[w for w, _ in squares], *[n for _, n in squares], *weights)  14.5 us
    unnamed x97, local copies, waits for them, and re-layouts  12.1 us
    pallas_call x4, Pallas kernels, local(): pl.pallas_call(functools.partial(eval_kernel, step), out_shape=jax.ShapeD...  11.5 us
  transfers between devices with their start and end apart: 39, of which 21 were waited for; matrix products, arithmetic and copies ran while one was open for 12% of the time, Pallas kernels for 25%

commit v1 on v0

v1 whole, which is shorter than its diff:
```python
import functools

import jax
import jax.numpy as jnp
from jax import lax
from jax.experimental import pallas as pl
from jax.experimental.pallas import tpu as pltpu
from jax.sharding import PartitionSpec as P

norm_eps = 1e-06
merge_eps = 1e-06
soft_cap = 30.0
gelu_coef = 0.7978845608028654
vmem_bytes = 56 * 1024 * 1024
bf16 = jnp.bfloat16
f32 = jnp.float32


def nt_dot(lhs, rhs):
    return lax.dot_general(lhs, rhs, (((1,), (1,)), ((), ())), preferred_element_type=f32)


def nn_dot(lhs, rhs):
    return lax.dot_general(lhs, rhs, (((1,), (0,)), ((), ())), preferred_element_type=f32)


def tn_dot(lhs, rhs):
    return lax.dot_general(lhs, rhs, (((0,), (0,)), ((), ())), preferred_element_type=f32)


def gelu_value(hidden):
    inner = gelu_coef * (hidden + 0.044715 * hidden * hidden * hidden)
    return 0.5 * hidden * (1.0 + jnp.tanh(inner))


def gelu_slope(hidden):
    inner = gelu_coef * (hidden + 0.044715 * hidden * hidden * hidden)
    tanh_value = jnp.tanh(inner)
    return 0.5 * (1.0 + tanh_value) + 0.5 * hidden * (1.0 - tanh_value * tanh_value) * gelu_coef * (
        1.0 + 3.0 * 0.044715 * hidden * hidden
    )


def row_scale(states):
    return lax.rsqrt(jnp.mean(states * states, axis=-1, keepdims=True) + norm_eps)


def square(values):
    wide = values.astype(f32)
    return (wide * wide).astype(bf16)


def label_head(states, labels, label_rows):
    wide = states.astype(f32)
    scale = row_scale(wide)
    norm_float = wide * scale
    logits = nt_dot(norm_float.astype(bf16), label_rows)
    bent = jnp.tanh(logits / soft_cap)
    capped = soft_cap * bent
    logprob = capped - jnp.log(jnp.sum(jnp.exp(capped), axis=-1, keepdims=True))
    one_hot = (labels == lax.broadcasted_iota(jnp.int32, logprob.shape, 1)).astype(f32)
    picked = jnp.sum(logprob * one_hot, axis=-1, keepdims=True)
    slope = ((jnp.exp(logprob) - one_hot) * (1.0 - bent * bent)).astype(bf16)
    grad_norm = nn_dot(slope, label_rows)
    mean = jnp.mean(grad_norm * norm_float, axis=-1, keepdims=True)
    return (scale * (grad_norm - norm_float * mean)).astype(bf16), picked


class Copies:
    def __init__(self, sems):
        self.sems, self.used = sems, 0

    def start(self, source, target):
        copy = pltpu.make_async_copy(source, target, self.sems.at[self.used])
        self.used += 1
        copy.start()
        return copy


class StageWeights:
    def __init__(self, member, own, other, held, sems):
        self.member, self.own, self.other = member, own, other
        self.held, self.sems = held, sems
        self.tasks = held[0].shape[1]

    def copy(self, kind, layer, task):
        return pltpu.make_async_copy(
            self.other[kind].at[task], self.held[kind].at[layer, task], self.sems.at[kind, layer, task]
        )

    def start(self, order):
        for kind, layer in order:
            @pl.when(self.member == layer)
            def _():
                for task in range(self.tasks):
                    pltpu.make_async_copy(
                        self.own[kind].at[layer * self.tasks + task],
                        self.held[kind].at[layer, task],
                        self.sems.at[kind, layer, task],
                    ).start()

            @pl.when(self.member != layer)
            def _():
                for task in range(self.tasks):
                    self.copy(kind, layer, task).start()

    def wait(self, kind, layer, task):
        self.copy(kind, layer, task).wait()


def forward_loop(levels, hidden, weights, held_down, held_up, done):
    tasks = levels.shape[1]

    @pl.loop(0, 2 * tasks)
    def _(index):
        layer, task = index // tasks, index % tasks
        wide = levels[layer, task].astype(f32)
        normed = (wide * row_scale(wide)).astype(bf16)
        weights.wait(0, layer, task)
        pre = nn_dot(normed, held_down[layer, task])
        hidden[layer, task] = pre
        active = gelu_value(pre).astype(bf16)
        weights.wait(1, layer, task)
        update = nt_dot(active, held_up[layer, task])
        levels[layer + 1, task] = (levels[layer, task].astype(f32) + update).astype(bf16)
        done(layer, task)


class Squares:
    def __init__(self, wide, narrow, wide_out, narrow_out, sems):
        self.pairs = ((wide, wide_out), (narrow, narrow_out))
        self.sems = sems

    def copy(self, width, layer, kind, task):
        source, target = self.pairs[width]
        return pltpu.make_async_copy(
            source.at[layer, kind, task], target.at[layer, kind, task], self.sems.at[width, layer, kind, task]
        )

    def keep(self, layer, kind, task, wide, narrow):
        self.pairs[0][0][layer, kind, task] = wide
        self.pairs[1][0][layer, kind, task] = narrow
        for width in range(2):
            self.copy(width, layer, kind, task).start()

    def wait(self):
        tasks = self.pairs[0][0].shape[2]

        @pl.loop(0, 2 * tasks)
        def _(index):
            for kind in range(2):
                for width in range(2):
                    self.copy(width, index // tasks, kind, index % tasks).wait()


def backward_step(layer, task, levels, grads, hidden, weights, held_down, held_up, squares, pass_on):
    grad = grads[layer + 1, task]
    pre = hidden[layer, task]
    if weights is not None:
        weights.wait(1, layer, task)
    grad_hidden = (nn_dot(grad, held_up[layer, task]) * gelu_slope(pre)).astype(bf16)
    if weights is not None and pass_on:
        weights.wait(0, layer, task)
    wide = levels[layer, task].astype(f32)
    scale = row_scale(wide)
    norm = wide * scale
    squares.keep(layer, 0, task, square(norm.astype(bf16)), square(grad_hidden))
    squares.keep(layer, 1, task, square(grad), square(gelu_value(pre).astype(bf16)))
    if pass_on:
        grad_norm = nt_dot(grad_hidden, held_down[layer, task])
        mean = jnp.mean(grad_norm * norm, axis=-1, keepdims=True)
        grads[layer, task] = (grad.astype(f32) + scale * (grad_norm - norm * mean)).astype(bf16)


def first_forward_kernel(turn, place, entry, down, up, down_other, up_other, out, middle, hidden,
                         levels, pre, sems, held_down, held_up, weight_sems):
    @pl.when(place[0] == 0)
    def _():
        tasks = out.shape[0]
        copies = Copies(sems)
        loads = [copies.start(entry.at[turn], levels.at[0, task]) for task in range(tasks)]
        weights = StageWeights(place[1], (down, up), (down_other, up_other), (held_down, held_up), weight_sems)
        weights.start([(0, 0), (1, 0), (0, 1), (1, 1)])
        for load in loads:
            load.wait()
        base = copies.used

        def leave(layer, task):
            return pltpu.make_async_copy(
                levels.at[layer + 1, task], (middle, out)[layer].at[task], sems.at[base + layer * tasks + task]
            )

        def done(layer, task):
            for fixed in range(2):
                @pl.when(layer == fixed)
                def _():
                    leave(fixed, task).start()

        forward_loop(levels, pre, weights, held_down, held_up, done)
        last = pltpu.make_async_copy(pre, hidden, sems.at[0])
        last.start()
        for layer in range(2):
            for task in range(tasks):
                leave(layer, task).wait()
        last.wait()


def first_backward_kernel(turn, place, grad, entry, middle, hidden, wide_in, narrow_in, down, up, down_other, up_other,
                          wide_out, narrow_out, grads, levels, pre, wide, narrow, square_sems, sems,
                          held_down, held_up, weight_sems):
    del wide_in, narrow_in

    @pl.when(place[0] == 0)
    def _():
        tasks = middle.shape[0]
        copies = Copies(sems)
        loads = [copies.start(grad, grads.at[2]), copies.start(hidden, pre), copies.start(middle, levels.at[1])]
        weights = StageWeights(place[1], (down, up), (down_other, up_other), (held_down, held_up), weight_sems)
        weights.start([(1, 1), (0, 1), (1, 0)])
        loads += [copies.start(entry.at[turn], levels.at[0, task]) for task in range(tasks)]
        squares = Squares(wide, narrow, wide_out, narrow_out, square_sems)
        for load in loads:
            load.wait()
        for layer in (1, 0):
            @pl.loop(0, tasks)
            def _(task):
                backward_step(
                    layer, task, levels, grads, pre, weights, held_down, held_up, squares, layer == 1
                )
        squares.wait()


def last_stage_kernel(turn, place, states, labels, label_rows, down, up, down_other, up_other,
                      grad_out, picked, wide_out, narrow_out,
                      levels, words, marks, chosen, pre, grads, wide, narrow, square_sems, sems,
                      held_down, held_up, weight_sems):
    @pl.when(place[0] == 1)
    def _():
        tasks, rows = states.shape[0], states.shape[1]
        copies = Copies(sems)
        loaded = copies.start(states, levels.at[0])
        weights = StageWeights(place[1], (down, up), (down_other, up_other), (held_down, held_up), weight_sems)
        weights.start([(0, 0), (1, 0), (0, 1), (1, 1)])
        later = [copies.start(label_rows, words), copies.start(labels.at[turn], marks)]
        loaded.wait()
        forward_loop(levels, pre, weights, held_down, held_up, lambda layer, task: None)
        for copy in later:
            copy.wait()

        @pl.loop(0, tasks)
        def _(task):
            grad, values = label_head(levels[2, task], marks[task], words[...])
            grads[2, task] = grad
            chosen[task] = jnp.broadcast_to(values, (rows, 128)).T[0:8]

        out_copy = copies.start(chosen, picked)
        squares = Squares(wide, narrow, wide_out, narrow_out, square_sems)

        @pl.loop(0, 2 * tasks)
        def _(index):
            backward_step(
                1 - index // tasks, index % tasks, levels, grads, pre, None, held_down, held_up, squares, True
            )

        last = copies.start(grads.at[0], grad_out)
        squares.wait()
        out_copy.wait()
        last.wait()


def eval_kernel(step, offsets, place, states, before, *refs):
    *pieces, out, base, top, held, sems = refs
    copies = Copies(sems)
    rows = pieces[0].shape[1]

    @pl.when(place[2] == step)
    def _():
        loads = [[copies.start(states, base)], [], []]
        for kind in range(2):
            for index, piece in enumerate(pieces):
                block = block_at(place[3], offsets[index], len(pieces))
                spot = pl.ds(pl.multiple_of(block * rows, 16), rows)
                loads[1 + kind].append(copies.start(piece.at[kind], held.at[kind, spot]))
        for load in loads[0]:
            load.wait()
        wide = base[...].astype(f32)
        normed = (wide * row_scale(wide)).astype(bf16)
        for load in loads[1]:
            load.wait()
        active = gelu_value(nn_dot(normed, held[0])).astype(bf16)
        for load in loads[2]:
            load.wait()
        top[...] = (wide + nt_dot(active, held[1])).astype(bf16)
        copies.start(top, out).wait()

    @pl.when(place[2] != step)
    def _():
        copies.start(before, base).wait()
        copies.start(base, out).wait()


def fisher_kernel(turns, place, *refs):
    wides, narrows = refs[:turns], refs[turns:2 * turns]
    own = refs[2 * turns:2 * turns + 2]
    other = refs[2 * turns + 2:2 * turns + 4]
    top_out, total_out, away_out = refs[2 * turns + 4:]
    member = place[1]
    tasks = own[0].shape[0]
    for slot in range(2):
        layer = member if slot == 0 else 1 - member
        weights = own if slot == 0 else other
        for kind in range(2):
            top, total = None, None
            for task in range(tasks):
                left = jnp.concatenate([ref[layer, kind, task] for ref in wides], axis=0)
                right = jnp.concatenate([ref[layer, kind, task] for ref in narrows], axis=0)
                term = tn_dot(left, right)
                scaled = term * weights[kind][task].astype(f32)
                top = scaled if top is None else top + scaled
                total = term if total is None else total + term
            if slot == 0:
                top_out[kind] = top.astype(bf16)
                total_out[kind] = total.astype(bf16)
            else:
                away_out[0, kind] = top.astype(bf16)
                away_out[1, kind] = total.astype(bf16)


def block_size(width):
    return max(size for size in range(128, 513, 128) if width % size == 0)


smem = pl.BlockSpec(memory_space=pltpu.SMEM)
hbm = pl.BlockSpec(memory_space=pl.ANY)


def send(block, axis, route):
    return lax.ppermute(block, axis, route)


def walk(spot, count):
    if count % 2:
        return spot
    return jnp.where(spot < count // 2, 2 * spot, 2 * (count - 1 - spot) + 1)


def spot_of(device, count):
    if count % 2:
        return device
    return jnp.where(lax.rem(device, 2) == 0, lax.div(device, 2), count - 1 - lax.div(device, 2))


def block_at(spot, offset, count):
    return walk(lax.rem(spot + offset + 2 * count, count), count)


def ring_routes(axis):
    count = lax.axis_size(axis)
    order = list(range(count)) if count % 2 else list(range(0, count, 2)) + list(range(count - 1, 0, -2))
    ahead = [(order[i], order[(i + 1) % count]) for i in range(count)]
    return count, ahead, [(j, i) for i, j in ahead]


def ring_scatter(own, other, spot, axis):
    count, ahead, back = ring_routes(axis)
    rows = own[0].shape[1] // count

    def part(index, offset):
        start = block_at(spot, offset, count) * rows
        mine = lax.dynamic_slice_in_dim(own[index], start, rows, 1)
        sizes = (1,) + mine.shape
        theirs = lax.dynamic_slice(other, (index, 0, start, 0), sizes).reshape(mine.shape)
        return mine.astype(f32) + theirs.astype(f32)

    moving = [part(0, -1).astype(bf16), part(1, 1).astype(bf16)]
    for step in range(count - 1):
        last = step == count - 2
        landed = [send(moving[0], axis, ahead), send(moving[1], axis, back)]
        sums = [landed[0].astype(f32) + part(0, -2 - step), landed[1].astype(f32) + part(1, 2 + step)]
        moving = sums if last else [value.astype(bf16) for value in sums]
    return moving


def ring_gather(own, axis):
    count, ahead, back = ring_routes(axis)
    pieces, offsets = [own], [0]
    down = up = own
    for step in range(1, count // 2 + 1):
        down = send(down, axis, ahead)
        pieces.append(down)
        offsets.append(-step)
        if len(pieces) < count:
            up = send(up, axis, back)
            pieces.append(up)
            offsets.append(step)
    return pieces, offsets


def after(value, done):
    return lax.optimization_barrier((value, done))[0]


def local(entry_states, down_proj, up_proj, label_rows, sampled_labels, eval_states):
    section_count = lax.axis_size("section")
    section = lax.axis_index("section")
    stage, member = section // 2, section % 2
    w_down, w_up = down_proj[0], up_proj[0]
    all_tasks, width, rank = w_down.shape
    tasks = all_tasks // 2
    micro, rows, _ = entry_states.shape
    label_count = label_rows.shape[0]
    spot = spot_of(lax.axis_index("dp"), lax.axis_size("dp"))
    place = jnp.stack([stage, member, section, spot]).astype(jnp.int32)
    sections = range(section_count)
    swap = [(i, i ^ 1) for i in sections]
    upward = [(i, i + 2) for i in sections if i + 2 < section_count]
    downward = [(i, i - 2) for i in sections if i - 2 >= 0]

    away = (1 - member) * tasks
    down_other = send(lax.dynamic_slice_in_dim(w_down, away, tasks, 0), "section", swap)
    up_other = send(lax.dynamic_slice_in_dim(w_up, away, tasks, 0), "section", swap)
    weights = (w_down, w_up, down_other, up_other)

    held = [
        pltpu.VMEM((2, tasks, width, rank), bf16),
        pltpu.VMEM((2, tasks, width, rank), bf16),
        pltpu.SemaphoreType.DMA((2, 2, tasks)),
    ]
    params = pltpu.CompilerParams(vmem_limit_bytes=vmem_bytes)
    state_shape, hidden_shape = (tasks, rows, width), (2, tasks, rows, rank)
    wide_shape, narrow_shape = (2, 2, tasks, rows, width), (2, 2, tasks, rows, rank)
    state_type = jax.ShapeDtypeStruct(state_shape, bf16)
    square_types = (jax.ShapeDtypeStruct(wide_shape, bf16), jax.ShapeDtypeStruct(narrow_shape, bf16))
    square_scratch = [
        pltpu.VMEM(wide_shape, bf16),
        pltpu.VMEM(narrow_shape, bf16),
        pltpu.SemaphoreType.DMA((2, 2, 2, tasks)),
    ]
    layer_flops = 4 * tasks * rows * width * rank
    weight_bytes = 8 * tasks * width * rank

    def stage_call(kernel, turn, name, operands, outputs, scratch, flops, **more):
        return pl.pallas_call(
            functools.partial(kernel, turn),
            out_shape=outputs,
            in_specs=[smem] + [hbm] * operands,
            out_specs=(hbm,) * len(outputs),
            scratch_shapes=scratch + held,
            compiler_params=params,
            cost_estimate=pl.CostEstimate(flops=flops, bytes_accessed=weight_bytes, transcendentals=0),
            name=name,
            **more,
        )

    own_labels = lax.dynamic_slice_in_dim(sampled_labels, member * tasks, tasks, 0)
    label_columns = own_labels.transpose(1, 0, 2).reshape(micro, tasks, rows, 1)
    saved, crossing, returned, picked = {}, {}, {}, {}
    squares = {}
    token = place

    levels, pre = pltpu.VMEM((3,) + state_shape, bf16), pltpu.VMEM(hidden_shape, f32)

    def first_forward(turn):
        nonlocal token
        call = stage_call(
            first_forward_kernel, turn, "first_forward", 5,
            (state_type, state_type, jax.ShapeDtypeStruct(hidden_shape, f32)),
            [levels, pre, pltpu.SemaphoreType.DMA((3 * tasks,))],
            2 * layer_flops,
        )
        out, middle, hidden = call(token, entry_states, *weights)
        saved[turn] = (entry_states, middle, hidden)
        crossing[turn] = out
        token = after(place, hidden)

    def cross(turn):
        nonlocal token
        out = lax.optimization_barrier((crossing[turn], token))[0]
        crossing[turn] = send(out, "section", upward)

    def last_stage(turn):
        nonlocal token
        call = stage_call(
            last_stage_kernel, turn, "last_stage", 7,
            (state_type, jax.ShapeDtypeStruct((tasks, 8, rows), f32)) + square_types,
            [
                levels, pltpu.VMEM(label_rows.shape, bf16),
                pltpu.VMEM((tasks, rows, 1), jnp.int32), pltpu.VMEM((tasks, 8, rows), f32),
                pre, levels,
            ] + square_scratch + [pltpu.SemaphoreType.DMA((5,))],
            4 * layer_flops + 4 * tasks * rows * width * label_count,
        )
        grad, picked[turn], *squares[turn] = call(
            token, crossing[turn], label_columns, label_rows, *weights
        )
        returned[turn] = send(grad, "section", downward)
        token = after(place, picked[turn])

    def first_backward(turn):
        nonlocal token
        call = stage_call(
            first_backward_kernel, turn, "first_backward", 10, square_types,
            [levels, levels, pre] + square_scratch + [pltpu.SemaphoreType.DMA((3 + tasks,))],
            2 * layer_flops,
            input_output_aliases={5: 0, 6: 1},
        )
        squares[turn] = call(token, returned[turn], *saved[turn], *squares[turn], *weights)
        token = after(place, squares[turn][1])

    ahead, behind = min(3, micro), 2
    for turn in range(ahead):
        first_forward(turn)
        cross(turn)
    for turn in range(micro):
        if turn + ahead < micro:
            first_forward(turn + ahead)
        if turn >= behind:
            first_backward(turn - behind)
            if turn + 1 in crossing:
                token = after(token, crossing[turn + 1])
        last_stage(turn)
        if turn + ahead < micro:
            cross(turn + ahead)
    picked_all = jnp.stack([picked[turn][:, 0] for turn in range(micro)], axis=0)
    label_logprob = jnp.zeros((micro, rows), f32)
    for index in range(tasks):
        route = [(section_count - 2 + m, m * tasks + index) for m in range(2)]
        landed = send(picked_all[:, index], "section", route)
        label_logprob = jnp.where(section % tasks == index, landed, label_logprob)

    token = after(place, label_logprob)
    for turn in range(max(micro - behind, 0), micro):
        first_backward(turn)

    block = block_size(width)

    def fisher(squares):
        turns = len(squares)
        call = pl.pallas_call(
            functools.partial(fisher_kernel, turns),
            out_shape=(jax.ShapeDtypeStruct((2, width, rank), bf16),) * 2
            + (jax.ShapeDtypeStruct((2, 2, width, rank), bf16),),
            grid_spec=pltpu.PrefetchScalarGridSpec(
                num_scalar_prefetch=1,
                grid=(width // block,),
                in_specs=[pl.BlockSpec((2, 2, tasks, rows, block), lambda i, s: (0, 0, 0, 0, i))] * turns
                + [pl.BlockSpec((2, 2, tasks, rows, rank), lambda i, s: (0, 0, 0, 0, 0))] * turns
                + [pl.BlockSpec((tasks, block, rank), lambda i, s: (s[1], i, 0))] * 2
                + [pl.BlockSpec((tasks, block, rank), lambda i, s: (0, i, 0))] * 2,
                out_specs=(pl.BlockSpec((2, block, rank), lambda i, s: (0, i, 0)),) * 2
                + (pl.BlockSpec((2, 2, block, rank), lambda i, s: (0, 0, i, 0)),),
            ),
            compiler_params=params,
            cost_estimate=pl.CostEstimate(
                flops=8 * tasks * turns * rows * width * rank,
                bytes_accessed=turns * 8 * tasks * rows * width,
                transcendentals=0,
            ),
            name="fisher",
        )
        return call(place, *[w for w, _ in squares], *[n for _, n in squares], *weights)

    *sums, away_sums = fisher([squares[turn] for turn in range(micro)])
    other_sums = send(away_sums, "section", swap)
    shares = ring_scatter(sums, other_sums, spot, "dp")
    numerator, denominator = shares
    merged_part = (numerator / (denominator + merge_eps)).astype(bf16)
    pieces, offsets = ring_gather(merged_part, "dp")
    fisher_log = jnp.log(denominator + merge_eps)

    current, result = eval_states, eval_states
    for step in range(section_count):
        result = pl.pallas_call(
            functools.partial(eval_kernel, step, offsets),
            out_shape=jax.ShapeDtypeStruct(eval_states.shape, bf16),
            in_specs=[smem] + [hbm] * (2 + len(pieces)),
            out_specs=hbm,
            scratch_shapes=[
                pltpu.VMEM(eval_states.shape, bf16), pltpu.VMEM(eval_states.shape, bf16),
                pltpu.VMEM((2, width, rank), bf16), pltpu.SemaphoreType.DMA((4 + 2 * len(pieces),)),
            ],
            compiler_params=pltpu.CompilerParams(vmem_limit_bytes=vmem_bytes),
            cost_estimate=pl.CostEstimate(
                flops=4 * eval_states.size * rank, bytes_accessed=4 * width * rank, transcendentals=0
            ),
            name="eval_block",
        )(place, current, result, *pieces)
        if step + 1 < section_count:
            current = send(result, "section", [(step, step + 1)])
    return (result[None], label_logprob[None], fisher_log[None])


def solution(mesh):
    placed = (
        P(None, "dp", None),
        P("section", None, None, None),
        P("section", None, None, None),
        P(),
        P(None, None, "dp"),
        P("dp", None),
    )
    return jax.shard_map(
        local,
        mesh=mesh,
        in_specs=placed,
        out_specs=(
            P("section", "dp", None),
            P("section", None, "dp"),
            P("section", None, "dp", None),
        ),
        check_vma=False,
    )
```

time: 362 us -> 352 us (0.972); the launches traced: 356 us -> 350 us
  waiting for transfers between devices: 89.7 us -> 147 us
  between operations: 23 us -> 1.49 us
  other arithmetic: 33.7 us -> 13.5 us
  local copies, waits for them, and re-layouts: 34.1 us -> 19.3 us
  starting transfers between devices: 57.1 us -> 44.2 us
  Pallas kernels: 119 us -> 125 us
    ppermute x39, waiting for transfers between devices: 89.7 us -> 147 us  [send(): return lax.ppermute(block, axis, route)]
    ppermute x39, starting transfers between devices: 57.1 us -> 44.2 us  [send(): return lax.ppermute(block, axis, route)]
    concatenate x15 -> x0, other arithmetic: 10.3 us -> none  [at_turn(): return jnp.concatenate([token, jnp.full((1,), turn, jnp.int32)])]
    another operation x7 -> x1, local copies, waits for them, and re-layouts: 6.62 us -> 0.01 us  [local(): jnp.stack([picked[turn][:, 0] for turn in range(micro)], axis=0)]
    convert_element_type x12 -> x6, other arithmetic: 14.6 us -> 9.12 us  [ring_scatter(): moving = sums if last else [value.astype(bf16) for value in sums]]
    pallas_call x5 -> x0, other arithmetic: 4.33 us -> none  [last_stage(): call(at_turn(turn), crossing[turn], label_columns, label_rows, *weights)]
    pallas_call x19, Pallas kernels: 104 us -> 108 us  [the longest x5 88 us: last_stage(): call(token, crossing[turn], label_columns, label_rows, *weights)]
    slice x2 -> x5, local copies, waits for them, and re-layouts: 7.45 us -> 3.49 us  [local(): picked[turn][:, 0]]
  transfers between devices with their start and end apart: 39 -> 39, of which waited for: 21 -> 25; matrix products, arithmetic and copies ran while one was open for 12% -> 2% of each run, Pallas kernels for 25% -> 27%
where the time goes in v1:
time: 352 us; the launch traced here: 350 us
  waiting for transfers between devices  147 us (42%)
  Pallas kernels  125 us (36%)
  starting transfers between devices  44.2 us (13%)
  local copies, waits for them, and re-layouts  19.3 us (5%)
  other arithmetic  13.5 us (4%)
    ppermute x39, waiting for transfers between devices, send(): return lax.ppermute(block, axis, route)  147 us
    pallas_call x5, Pallas kernels, last_stage(): call(token, crossing[turn], label_columns, label_rows, *weights)  88 us
    ppermute x39, starting transfers between devices, send(): return lax.ppermute(block, axis, route)  44.2 us
    pallas_call x1, Pallas kernels, fisher(): call(place, *[w for w, _ in squares], *[n for _, n in squares], *weights)  16.7 us
    pallas_call x4, Pallas kernels, local(): pl.pallas_call(functools.partial(eval_kernel, step, offsets), out_shape=j...  11.5 us
    unnamed x63, local copies, waits for them, and re-layouts  10 us
    convert_element_type x6, other arithmetic, ring_scatter(): moving = sums if last else [value.astype(bf16) for value in sums]  9.12 us
  transfers between devices with their start and end apart: 39, of which 25 were waited for; matrix products, arithmetic and copies ran while one was open for 2% of the time, Pallas kernels for 27%

profile of v1, /device:TPU:23, one launch (start us, length us, event | category | flops | bytes accessed | tf_op | source)
XLA Modules:
  0.0 350.4 jit_solution(4062420859923096469)
XLA Ops:
  0.7 3.4 dynamic-slice_bitcast_fusion.1
  4.7 1.6 dynamic-slice_bitcast_fusion
  6.9 2.2 collective-permute-done.down_other.refs_12_
  9.1 3.5 collective-permute-done.1.up_other.refs_13_
  13.4 1.3 collective-permute-start.2
  15.5 1.3 collective-permute-start.3
  19.3 17.7 %collective-permute-done.2.states = bf16[2,32,4608]{2,1,0:T(8,128)(2,1)S(1)} collective-permute-done((bf16[2,32,4608]{2,1,0:T(8,128)(2,1)}, bf16[2,32,4608]{2,1,0:T(8,128)(2,1)S(1)}, u32[]{:S(2)}, u32[]{:S(2)}) %collective-permute-start.2) | collective-permute-done | bytes 589856 | tf_op jit(solution)/shard_map/ppermute | solution.py:338
  37.8 17.6 %last_stage.5 = (bf16[2,32,4608]{2,1,0:T(8,128)(2,1)}, f32[2,8,32]{2,1,0:T(8,128)}, bf16[2,2,2,32,4608]{4,3,2,1,0:T(8,128)(2,1)}, bf16[2,2,2,32,128]{4,3,2,1,0:T(8,128)(2,1)}) custom-call(s32[4]{0:T(128)} %pad_add_fusion.place, bf16[2,32,4608]{2,1,0:T(8,128)(2,1)} %copy-done.21, s32[5,2,32,1]{3,2,1,0:T(8,128)} %copy.21.labels, bf16[256,4608]{1,0:T(8,128)(2,1)} %label_rows.9, ...), custom_call_target="tpu_custom_call" | custom-call | flops 905969664 | bytes 9437184 | tf_op jit(solution)/shard_map/last_stage/pallas_call | solution.py:493
  55.3 2.1 collective-permute-start.4
  57.4 1.3 collective-permute-start.5
  58.7 1.3 collective-permute-start.6
  61.7 17.6 %last_stage.6 = (bf16[2,32,4608]{2,1,0:T(8,128)(2,1)}, f32[2,8,32]{2,1,0:T(8,128)}, bf16[2,2,2,32,4608]{4,3,2,1,0:T(8,128)(2,1)}, bf16[2,2,2,32,128]{4,3,2,1,0:T(8,128)(2,1)}) custom-call(s32[4]{0:T(128)} %pad_add_fusion.place, bf16[2,32,4608]{2,1,0:T(8,128)(2,1)} %copy-done.18, s32[5,2,32,1]{3,2,1,0:T(8,128)} %copy.21.labels, bf16[256,4608]{1,0:T(8,128)(2,1)} %label_rows.9, ...), custom_call_target="tpu_custom_call" | custom-call | flops 905969664 | bytes 9437184 | tf_op jit(solution)/shard_map/last_stage/pallas_call | solution.py:493
  79.3 1.3 collective-permute-start.7
  80.6 1.3 collective-permute-start.8
  83.7 2.3 collective-permute-done.6.states
  86.8 17.7 %last_stage.7 = (bf16[2,32,4608]{2,1,0:T(8,128)(2,1)}, f32[2,8,32]{2,1,0:T(8,128)}, bf16[2,2,2,32,4608]{4,3,2,1,0:T(8,128)(2,1)}, bf16[2,2,2,32,128]{4,3,2,1,0:T(8,128)(2,1)}) custom-call(s32[4]{0:T(128)} %pad_add_fusion.place, bf16[2,32,4608]{2,1,0:T(8,128)(2,1)} %copy-done.19, s32[5,2,32,1]{3,2,1,0:T(8,128)} %copy.21.labels, bf16[256,4608]{1,0:T(8,128)(2,1)} %label_rows.9, ...), custom_call_target="tpu_custom_call" | custom-call | flops 905969664 | bytes 9437184 | tf_op jit(solution)/shard_map/last_stage/pallas_call | solution.py:493
  104.6 1.3 collective-permute-start.9
  109.8 17.6 %last_stage.8 = (bf16[2,32,4608]{2,1,0:T(8,128)(2,1)}, f32[2,8,32]{2,1,0:T(8,128)}, bf16[2,2,2,32,4608]{4,3,2,1,0:T(8,128)(2,1)}, bf16[2,2,2,32,128]{4,3,2,1,0:T(8,128)(2,1)}) custom-call(s32[4]{0:T(128)} %pad_add_fusion.place, bf16[2,32,4608]{2,1,0:T(8,128)(2,1)} %copy-done.13, s32[5,2,32,1]{3,2,1,0:T(8,128)} %copy.21.labels, bf16[256,4608]{1,0:T(8,128)(2,1)} %label_rows.9, ...), custom_call_target="tpu_custom_call" | custom-call | flops 905969664 | bytes 9437184 | tf_op jit(solution)/shard_map/last_stage/pallas_call | solution.py:493
  128.1 1.3 collective-permute-start.12
  131.2 17.5 %last_stage.9 = (bf16[2,32,4608]{2,1,0:T(8,128)(2,1)}, f32[2,8,32]{2,1,0:T(8,128)}, bf16[2,2,2,32,4608]{4,3,2,1,0:T(8,128)(2,1)}, bf16[2,2,2,32,128]{4,3,2,1,0:T(8,128)(2,1)}) custom-call(s32[4]{0:T(128)} %pad_add_fusion.place, bf16[2,32,4608]{2,1,0:T(8,128)(2,1)} %copy-done.12, s32[5,2,32,1]{3,2,1,0:T(8,128)} %copy.21.labels, bf16[256,4608]{1,0:T(8,128)(2,1)} %label_rows.9, ...), custom_call_target="tpu_custom_call" | custom-call | flops 905969664 | bytes 9437184 | tf_op jit(solution)/shard_map/last_stage/pallas_call | solution.py:493
  149.4 1.3 collective-permute-start.13
  151.5 4.6 %collective-permute-start.11 = (f32[5,32]{1,0:T(8,128)S(1)}, f32[5,32]{1,0:T(8,128)S(1)}, u32[]{:S(2)}, u32[]{:S(2)}) collective-permute-start(f32[5,32]{1,0:T(8,128)S(1)} %bitcast.118), channel_id=1, source_target_pairs={{16,0},{24,16},{17,1},{25,17},{18,2},{26,18},{19,3},{27,19},{20,4}... | collective-permute-start | bytes 1928 | tf_op jit(solution)/shard_map/ppermute | solution.py:338
  157.7 1.1 first_backward.8
  158.9 3.0 collective-permute-done.13.grad
  163.6 16.7 %fisher.1 = (bf16[2,4608,128]{2,1,0:T(8,128)(2,1)}, bf16[2,4608,128]{2,1,0:T(8,128)(2,1)}, bf16[2,2,4608,128]{3,2,1,0:T(8,128)(2,1)}) custom-call(s32[4]{0:T(128)} %pad_add_fusion.place, bf16[2,2,2,32,4608]{4,3,2,1,0:T(8,128)(2,1)} %get-tuple-element.94.refs_0_, bf16[2,2,2,32,4608]{4,3,2,1,0:T(8,128)(2,1)} %get-tuple-element.108.refs_1_, ...), custom_call_target="tpu_custom_call" | custom-call | flops 1509949440 | bytes 11796480 | tf_op jit(solution)/shard_map/fisher/pallas_call | solution.py:561
  180.4 4.8 %collective-permute-start.14 = (bf16[2,2,4608,128]{3,2,1,0:T(8,128)(2,1)}, bf16[2,2,4608,128]{3,2,1,0:T(8,128)(2,1)}, u32[]{:S(2)}, u32[]{:S(2)}) collective-permute-start(bf16[2,2,4608,128]{3,2,1,0:T(8,128)(2,1)} %get-tuple-element.139), channel_id=1, source_target_pairs={{0,8},{8,0},{16,24},{24,16},{1,9},{9,1},{17,25},{25,17},{2,10},{10... | collective-permute-start | bytes 14155784 | tf_op jit(solution)/shard_map/ppermute | solution.py:338
  185.1 7.9 %collective-permute-done.14 = bf16[2,2,4608,128]{3,2,1,0:T(8,128)(2,1)} collective-permute-done((bf16[2,2,4608,128]{3,2,1,0:T(8,128)(2,1)}, bf16[2,2,4608,128]{3,2,1,0:T(8,128)(2,1)}, u32[]{:S(2)}, u32[]{:S(2)}) %collective-permute-start.14) | collective-permute-done | bytes 4718624 | tf_op jit(solution)/shard_map/ppermute | solution.py:338
  193.0 1.4 fusion.14
  194.6 1.3 collective-permute-start.22
  195.9 6.8 %collective-permute-done.15 = bf16[2,576,128]{2,1,0:T(8,128)(2,1)S(1)} collective-permute-done((bf16[2,576,128]{2,1,0:T(8,128)(2,1)S(1)}, bf16[2,576,128]{2,1,0:T(8,128)(2,1)S(1)}, u32[]{:S(2)}, u32[]{:S(2)}) %collective-permute-start.15) | collective-permute-done | bytes 294944 | tf_op jit(solution)/shard_map/ppermute | solution.py:338
  202.7 1.5 fusion.13
  204.4 1.3 collective-permute-start.23
  205.7 5.7 %collective-permute-done.16 = bf16[2,576,128]{2,1,0:T(8,128)(2,1)S(1)} collective-permute-done((bf16[2,576,128]{2,1,0:T(8,128)(2,1)S(1)}, bf16[2,576,128]{2,1,0:T(8,128)(2,1)S(1)}, u32[]{:S(2)}, u32[]{:S(2)}) %collective-permute-start.16) | collective-permute-done | bytes 294944 | tf_op jit(solution)/shard_map/ppermute | solution.py:338
  211.4 1.5 fusion.11
  213.3 1.2 collective-permute-start.24
  214.4 4.6 %collective-permute-done.17 = bf16[2,576,128]{2,1,0:T(8,128)(2,1)S(1)} collective-permute-done((bf16[2,576,128]{2,1,0:T(8,128)(2,1)S(1)}, bf16[2,576,128]{2,1,0:T(8,128)(2,1)S(1)}, u32[]{:S(2)}, u32[]{:S(2)}) %collective-permute-start.17) | collective-permute-done | bytes 294944 | tf_op jit(solution)/shard_map/ppermute | solution.py:338
  219.1 1.5 fusion.9
  222.2 4.1 %collective-permute-done.18 = bf16[2,576,128]{2,1,0:T(8,128)(2,1)S(1)} collective-permute-done((bf16[2,576,128]{2,1,0:T(8,128)(2,1)S(1)}, bf16[2,576,128]{2,1,0:T(8,128)(2,1)S(1)}, u32[]{:S(2)}, u32[]{:S(2)}) %collective-permute-start.18) | collective-permute-done | bytes 294944 | tf_op jit(solution)/shard_map/ppermute | solution.py:338
  227.1 1.5 fusion.7
  228.6 1.6 collective-permute-start.19
  230.3 4.0 %collective-permute-done.19 = bf16[2,576,128]{2,1,0:T(8,128)(2,1)S(1)} collective-permute-done((bf16[2,576,128]{2,1,0:T(8,128)(2,1)S(1)}, bf16[2,576,128]{2,1,0:T(8,128)(2,1)S(1)}, u32[]{:S(2)}, u32[]{:S(2)}) %collective-permute-start.19) | collective-permute-done | bytes 294944 | tf_op jit(solution)/shard_map/ppermute | solution.py:338
  234.2 1.6 collective-permute-done.26
  235.8 1.5 fusion.5
  237.4 1.4 collective-permute-start.20
  238.9 4.3 %collective-permute-done.20 = bf16[2,576,128]{2,1,0:T(8,128)(2,1)S(1)} collective-permute-done((bf16[2,576,128]{2,1,0:T(8,128)(2,1)S(1)}, bf16[2,576,128]{2,1,0:T(8,128)(2,1)S(1)}, u32[]{:S(2)}, u32[]{:S(2)}) %collective-permute-start.20) | collective-permute-done | bytes 294944 | tf_op jit(solution)/shard_map/ppermute | solution.py:338
  243.2 1.6 collective-permute-done.27
  244.7 1.5 fusion.3
  246.3 1.4 collective-permute-start.21
  247.8 5.9 %collective-permute-done.21 = bf16[2,576,128]{2,1,0:T(8,128)(2,1)S(1)} collective-permute-done((bf16[2,576,128]{2,1,0:T(8,128)(2,1)S(1)}, bf16[2,576,128]{2,1,0:T(8,128)(2,1)S(1)}, u32[]{:S(2)}, u32[]{:S(2)}) %collective-permute-start.21) | collective-permute-done | bytes 294944 | tf_op jit(solution)/shard_map/ppermute | solution.py:338
  253.7 1.8 collective-permute-done.28
  255.5 2.4 log_bitcast_fusion
  257.9 1.7 collective-permute-start.29
  259.7 6.8 %collective-permute-done.29.refs_1_ = bf16[2,576,128]{2,1,0:T(8,128)(2,1)S(1)} collective-permute-done((bf16[2,576,128]{2,1,0:T(8,128)(2,1)S(1)}, bf16[2,576,128]{2,1,0:T(8,128)(2,1)S(1)}, u32[]{:S(2)}, u32[]{:S(2)}) %collective-permute-start.29) | collective-permute-done | bytes 294944 | tf_op jit(solution)/shard_map/ppermute | solution.py:338
  266.5 2.2 collective-permute-start.31
  268.7 3.7 %collective-permute-done.31.refs_3_ = bf16[2,576,128]{2,1,0:T(8,128)(2,1)S(1)} collective-permute-done((bf16[2,576,128]{2,1,0:T(8,128)(2,1)S(1)}, bf16[2,576,128]{2,1,0:T(8,128)(2,1)S(1)}, u32[]{:S(2)}, u32[]{:S(2)}) %collective-permute-start.31) | collective-permute-done | bytes 294944 | tf_op jit(solution)/shard_map/ppermute | solution.py:338
  272.4 1.9 collective-permute-start.33
  274.3 6.4 %collective-permute-done.33.refs_5_ = bf16[2,576,128]{2,1,0:T(8,128)(2,1)S(1)} collective-permute-done((bf16[2,576,128]{2,1,0:T(8,128)(2,1)S(1)}, bf16[2,576,128]{2,1,0:T(8,128)(2,1)S(1)}, u32[]{:S(2)}, u32[]{:S(2)}) %collective-permute-start.33) | collective-permute-done | bytes 294944 | tf_op jit(solution)/shard_map/ppermute | solution.py:338
  281.4 7.5 %collective-permute-done.35.refs_7_ = bf16[2,576,128]{2,1,0:T(8,128)(2,1)S(1)} collective-permute-done((bf16[2,576,128]{2,1,0:T(8,128)(2,1)S(1)}, bf16[2,576,128]{2,1,0:T(8,128)(2,1)S(1)}, u32[]{:S(2)}, u32[]{:S(2)}) %collective-permute-start.35) | collective-permute-done | bytes 294944 | tf_op jit(solution)/shard_map/ppermute | solution.py:338
  289.7 2.5 eval_block.4.before
  293.7 2.5 eval_block.5.before
  297.6 2.7 eval_block.6.before
  300.3 1.3 collective-permute-start.38
  302.2 43.6 %collective-permute-done.38.states = bf16[32,4608]{1,0:T(8,128)(2,1)S(1)} collective-permute-done((bf16[32,4608]{1,0:T(8,128)(2,1)}, bf16[32,4608]{1,0:T(8,128)(2,1)S(1)}, u32[]{:S(2)}, u32[]{:S(2)}) %collective-permute-start.38) | collective-permute-done | bytes 294944 | tf_op jit(solution)/shard_map/ppermute | solution.py:338
  346.5 3.8 %eval_block.7 = bf16[32,4608]{1,0:T(8,128)(2,1)} custom-call(s32[4]{0:T(128)} %pad_add_fusion.place, bf16[32,4608]{1,0:T(8,128)(2,1)} %copy-done.22, bf16[32,4608]{1,0:T(8,128)(2,1)} %eval_block.6.before, bf16[2,576,128]{2,1,0:T(8,128)(2,1)} %copy-done.4, bf16[2,576,128]{2,1,0:T(8,128)(2,1)} %copy-done.5, bf16[2,576,128]{2,1,0:T(8,128)(2,1)} %copy-done.6, ...), custom_call_target="tpu_custom_call" | custom-call | flops 75497472 | bytes 2359296 | tf_op jit(solution)/shard_map/eval_block/pallas_call | solution.py:573
  (118 shorter events, 30.5 us)
Async XLA Ops:
  0.6 16.2 %copy-start = (s32[4,5,32]{2,0,1:T(4,128)S(1)}, s32[4,5,32]{2,0,1:T(4,128)}, u32[]{:S(2)}) copy-start(s32[4,5,32]{2,0,1:T(4,128)} %param.10) | copy-start | bytes 7684
  0.7 4.1 %copy-start.2 = (bf16[1,4,4608,128]{3,2,1,0:T(8,128)(2,1)S(1)}, bf16[1,4,4608,128]{3,2,1,0:T(8,128)(2,1)}, u32[]{:S(2)}) copy-start(bf16[1,4,4608,128]{3,2,1,0:T(8,128)(2,1)} %param.8) | copy-start | bytes 14155780
  4.1 5.0 %collective-permute-start = (bf16[2,4608,128]{2,1,0:T(8,128)(2,1)}, bf16[2,4608,128]{2,1,0:T(8,128)(2,1)S(1)}, u32[]{:S(2)}, u32[]{:S(2)}) collective-permute-start(bf16[2,4608,128]{2,1,0:T(8,128)(2,1)} %dynamic-slice_bitcast_fusion.1), channel_id=1, source_target_pairs={{0,8},{8,0},{16,24},{24,16},{1,9},{9,1},{17,25},{25,17},{2,10},{10... | collective-permute-start | bytes 7077896 | tf_op jit(solution)/shard_map/ppermute | solution.py:338
  6.3 6.3 %collective-permute-start.1 = (bf16[2,4608,128]{2,1,0:T(8,128)(2,1)}, bf16[2,4608,128]{2,1,0:T(8,128)(2,1)}, u32[]{:S(2)}, u32[]{:S(2)}) collective-permute-start(bf16[2,4608,128]{2,1,0:T(8,128)(2,1)} %dynamic-slice_bitcast_fusion), channel_id=1, source_target_pairs={{0,8},{8,0},{16,24},{24,16},{1,9},{9,1},{17,25},{25,17},{2,10},{10... | collective-permute-start | bytes 7077896 | tf_op jit(solution)/shard_map/ppermute | solution.py:338
  9.1 3.5 %copy-start.3 = (bf16[2,4608,128]{2,1,0:T(8,128)(2,1)}, bf16[2,4608,128]{2,1,0:T(8,128)(2,1)S(1)}, u32[]{:S(2)}) copy-start(bf16[2,4608,128]{2,1,0:T(8,128)(2,1)S(1)} %collective-permute-done.down_other.refs_12_) | copy-start | bytes 7077892
  13.4 23.5 %collective-permute-start.2 = (bf16[2,32,4608]{2,1,0:T(8,128)(2,1)}, bf16[2,32,4608]{2,1,0:T(8,128)(2,1)S(1)}, u32[]{:S(2)}, u32[]{:S(2)}) collective-permute-start(bf16[2,32,4608]{2,1,0:T(8,128)(2,1)} %get-tuple-element.81), channel_id=1, source_target_pairs={{0,16},{8,24},{1,17},{9,25},{2,18},{10,26},{3,19},{11,27},{4,20},{... | collective-permute-start | bytes 1769480 | tf_op jit(solution)/shard_map/ppermute | solution.py:338
  15.5 45.3 %collective-permute-start.3 = (bf16[2,32,4608]{2,1,0:T(8,128)(2,1)}, bf16[2,32,4608]{2,1,0:T(8,128)(2,1)S(1)}, u32[]{:S(2)}, u32[]{:S(2)}) collective-permute-start(bf16[2,32,4608]{2,1,0:T(8,128)(2,1)} %get-tuple-element.87), channel_id=1, source_target_pairs={{0,16},{8,24},{1,17},{9,25},{2,18},{10,26},{3,19},{11,27},{4,20},{... | collective-permute-start | bytes 1769480 | tf_op jit(solution)/shard_map/ppermute | solution.py:338
  19.3 38.1 %copy-start.27 = (bf16[2,32,4608]{2,1,0:T(8,128)(2,1)S(1)}, bf16[2,32,4608]{2,1,0:T(8,128)(2,1)}, u32[]{:S(2)}) copy-start(bf16[2,32,4608]{2,1,0:T(8,128)(2,1)} %get-tuple-element.98) | copy-start | bytes 1769476
  19.3 39.4 %copy-start.26 = (bf16[2,32,4608]{2,1,0:T(8,128)(2,1)S(1)}, bf16[2,32,4608]{2,1,0:T(8,128)(2,1)}, u32[]{:S(2)}) copy-start(bf16[2,32,4608]{2,1,0:T(8,128)(2,1)} %get-tuple-element.101) | copy-start | bytes 1769476
  37.0 0.8 copy-start.21
  55.3 26.6 %collective-permute-start.4 = (bf16[2,32,4608]{2,1,0:T(8,128)(2,1)}, bf16[2,32,4608]{2,1,0:T(8,128)(2,1)S(1)}, u32[]{:S(2)}, u32[]{:S(2)}) collective-permute-start(bf16[2,32,4608]{2,1,0:T(8,128)(2,1)} %get-tuple-element.90), channel_id=1, source_target_pairs={{16,0},{24,8},{17,1},{25,9},{18,2},{26,10},{19,3},{27,11},{20,4},{... | collective-permute-start | bytes 1769480 | tf_op jit(solution)/shard_map/ppermute | solution.py:338
  57.4 26.3 %collective-permute-start.5 = (bf16[2,32,4608]{2,1,0:T(8,128)(2,1)S(1)}, bf16[2,32,4608]{2,1,0:T(8,128)(2,1)S(1)}, u32[]{:S(2)}, u32[]{:S(2)}) collective-permute-start(bf16[2,32,4608]{2,1,0:T(8,128)(2,1)S(1)} %copy-done.27), channel_id=1, source_target_pairs={{0,16},{8,24},{1,17},{9,25},{2,18},{10,26},{3,19},{11,27},{4,20},{... | collective-permute-start | bytes 1769480 | tf_op jit(solution)/shard_map/ppermute | solution.py:338
  58.7 27.2 %collective-permute-start.6 = (bf16[2,32,4608]{2,1,0:T(8,128)(2,1)S(1)}, bf16[2,32,4608]{2,1,0:T(8,128)(2,1)S(1)}, u32[]{:S(2)}, u32[]{:S(2)}) collective-permute-start(bf16[2,32,4608]{2,1,0:T(8,128)(2,1)S(1)} %copy-done.26), channel_id=1, source_target_pairs={{0,16},{8,24},{1,17},{9,25},{2,18},{10,26},{3,19},{11,27},{4,20},{... | collective-permute-start | bytes 1769480 | tf_op jit(solution)/shard_map/ppermute | solution.py:338
  60.9 19.8 %copy-start.25 = (bf16[2,32,4608]{2,1,0:T(8,128)(2,1)S(1)}, bf16[2,32,4608]{2,1,0:T(8,128)(2,1)}, u32[]{:S(2)}) copy-start(bf16[2,32,4608]{2,1,0:T(8,128)(2,1)} %get-tuple-element.112) | copy-start | bytes 1769476
  60.9 0.8 copy-start.18
  79.3 28.7 %collective-permute-start.7 = (bf16[2,32,4608]{2,1,0:T(8,128)(2,1)}, bf16[2,32,4608]{2,1,0:T(8,128)(2,1)S(1)}, u32[]{:S(2)}, u32[]{:S(2)}) collective-permute-start(bf16[2,32,4608]{2,1,0:T(8,128)(2,1)} %get-tuple-element.104), channel_id=1, source_target_pairs={{16,0},{24,8},{17,1},{25,9},{18,2},{26,10},{19,3},{27,11},{20,4},{... | collective-permute-start | bytes 1769480 | tf_op jit(solution)/shard_map/ppermute | solution.py:338
  80.6 29.1 %collective-permute-start.8 = (bf16[2,32,4608]{2,1,0:T(8,128)(2,1)S(1)}, bf16[2,32,4608]{2,1,0:T(8,128)(2,1)S(1)}, u32[]{:S(2)}, u32[]{:S(2)}) collective-permute-start(bf16[2,32,4608]{2,1,0:T(8,128)(2,1)S(1)} %copy-done.25), channel_id=1, source_target_pairs={{0,16},{8,24},{1,17},{9,25},{2,18},{10,26},{3,19},{11,27},{4,20},{... | collective-permute-start | bytes 1769480 | tf_op jit(solution)/shard_map/ppermute | solution.py:338
  81.9 0.8 copy-start.20
  83.7 20.8 %copy-start.13 = (bf16[2,32,4608]{2,1,0:T(8,128)(2,1)}, bf16[2,32,4608]{2,1,0:T(8,128)(2,1)S(1)}, u32[]{:S(2)}) copy-start(bf16[2,32,4608]{2,1,0:T(8,128)(2,1)S(1)} %collective-permute-done.5.states) | copy-start | bytes 1769476
  86.0 0.8 copy-start.19
  104.6 24.9 %collective-permute-start.9 = (bf16[2,32,4608]{2,1,0:T(8,128)(2,1)}, bf16[2,32,4608]{2,1,0:T(8,128)(2,1)S(1)}, u32[]{:S(2)}, u32[]{:S(2)}) collective-permute-start(bf16[2,32,4608]{2,1,0:T(8,128)(2,1)} %get-tuple-element.116), channel_id=1, source_target_pairs={{16,0},{24,8},{17,1},{25,9},{18,2},{26,10},{19,3},{27,11},{20,4},{... | collective-permute-start | bytes 1769480 | tf_op jit(solution)/shard_map/ppermute | solution.py:338
  108.0 0.8 copy-start.16
  109.8 17.6 %copy-start.12 = (bf16[2,32,4608]{2,1,0:T(8,128)(2,1)}, bf16[2,32,4608]{2,1,0:T(8,128)(2,1)S(1)}, u32[]{:S(2)}) copy-start(bf16[2,32,4608]{2,1,0:T(8,128)(2,1)S(1)} %collective-permute-done.8.states) | copy-start | bytes 1769476
  128.1 28.8 %collective-permute-start.12 = (bf16[2,32,4608]{2,1,0:T(8,128)(2,1)}, bf16[2,32,4608]{2,1,0:T(8,128)(2,1)S(1)}, u32[]{:S(2)}, u32[]{:S(2)}) collective-permute-start(bf16[2,32,4608]{2,1,0:T(8,128)(2,1)} %get-tuple-element.125), channel_id=1, source_target_pairs={{16,0},{24,8},{17,1},{25,9},{18,2},{26,10},{19,3},{27,11},{20,4},{... | collective-permute-start | bytes 1769480 | tf_op jit(solution)/shard_map/ppermute | solution.py:338
  129.4 0.8 copy-start.17
  149.4 12.4 %collective-permute-start.13 = (bf16[2,32,4608]{2,1,0:T(8,128)(2,1)}, bf16[2,32,4608]{2,1,0:T(8,128)(2,1)S(1)}, u32[]{:S(2)}, u32[]{:S(2)}) collective-permute-start(bf16[2,32,4608]{2,1,0:T(8,128)(2,1)} %get-tuple-element.132), channel_id=1, source_target_pairs={{16,0},{24,8},{17,1},{25,9},{18,2},{26,10},{19,3},{27,11},{20,4},{... | collective-permute-start | bytes 1769480 | tf_op jit(solution)/shard_map/ppermute | solution.py:338
  150.8 5.3 %collective-permute-start.10 = (f32[5,32]{1,0:T(8,128)S(1)}, f32[5,32]{1,0:T(8,128)S(1)}, u32[]{:S(2)}, u32[]{:S(2)}) collective-permute-start(f32[5,32]{1,0:T(8,128)S(1)} %bitcast.117), channel_id=1, source_target_pairs={{16,8},{24,24},{17,9},{25,25},{18,10},{26,26},{19,11},{27,27},{20,... | collective-permute-start | bytes 1928 | tf_op jit(solution)/shard_map/ppermute | solution.py:338
  151.5 5.4 %collective-permute-start.11 = (f32[5,32]{1,0:T(8,128)S(1)}, f32[5,32]{1,0:T(8,128)S(1)}, u32[]{:S(2)}, u32[]{:S(2)}) collective-permute-start(f32[5,32]{1,0:T(8,128)S(1)} %bitcast.118), channel_id=1, source_target_pairs={{16,0},{24,16},{17,1},{25,17},{18,2},{26,18},{19,3},{27,19},{20,4}... | collective-permute-start | bytes 1928 | tf_op jit(solution)/shard_map/ppermute | solution.py:338
  156.9 0.8 copy-start.14
  161.9 0.8 copy-start.15
  180.4 12.6 %collective-permute-start.14 = (bf16[2,2,4608,128]{3,2,1,0:T(8,128)(2,1)}, bf16[2,2,4608,128]{3,2,1,0:T(8,128)(2,1)}, u32[]{:S(2)}, u32[]{:S(2)}) collective-permute-start(bf16[2,2,4608,128]{3,2,1,0:T(8,128)(2,1)} %get-tuple-element.139), channel_id=1, source_target_pairs={{0,8},{8,0},{16,24},{24,16},{1,9},{9,1},{17,25},{25,17},{2,10},{10... | collective-permute-start | bytes 14155784 | tf_op jit(solution)/shard_map/ppermute | solution.py:338
  194.4 8.3 %collective-permute-start.15 = (bf16[2,576,128]{2,1,0:T(8,128)(2,1)S(1)}, bf16[2,576,128]{2,1,0:T(8,128)(2,1)S(1)}, u32[]{:S(2)}, u32[]{:S(2)}) collective-permute-start(bf16[2,576,128]{2,1,0:T(8,128)(2,1)S(1)} %get-tuple-element.162), channel_id=1, source_target_pairs={{0,2},{2,4},{4,6},{6,7},{7,5},{5,3},{3,1},{1,0},{8,10},{10,12},{12... | collective-permute-start | bytes 884744 | tf_op jit(solution)/shard_map/ppermute | solution.py:338
  194.6 8.1 %collective-permute-start.22 = (bf16[2,576,128]{2,1,0:T(8,128)(2,1)S(1)}, bf16[2,576,128]{2,1,0:T(8,128)(2,1)S(1)}, u32[]{:S(2)}, u32[]{:S(2)}) collective-permute-start(bf16[2,576,128]{2,1,0:T(8,128)(2,1)S(1)} %get-tuple-element.161), channel_id=1, source_target_pairs={{2,0},{4,2},{6,4},{7,6},{5,7},{3,5},{1,3},{0,1},{10,8},{12,10},{14... | collective-permute-start | bytes 884744 | tf_op jit(solution)/shard_map/ppermute | solution.py:338
  204.2 7.2 %collective-permute-start.16 = (bf16[2,576,128]{2,1,0:T(8,128)(2,1)S(1)}, bf16[2,576,128]{2,1,0:T(8,128)(2,1)S(1)}, u32[]{:S(2)}, u32[]{:S(2)}) collective-permute-start(bf16[2,576,128]{2,1,0:T(8,128)(2,1)S(1)} %get-tuple-element.160), channel_id=1, source_target_pairs={{0,2},{2,4},{4,6},{6,7},{7,5},{5,3},{3,1},{1,0},{8,10},{10,12},{12... | collective-permute-start | bytes 884744 | tf_op jit(solution)/shard_map/ppermute | solution.py:338
  204.4 7.0 %collective-permute-start.23 = (bf16[2,576,128]{2,1,0:T(8,128)(2,1)S(1)}, bf16[2,576,128]{2,1,0:T(8,128)(2,1)S(1)}, u32[]{:S(2)}, u32[]{:S(2)}) collective-permute-start(bf16[2,576,128]{2,1,0:T(8,128)(2,1)S(1)} %get-tuple-element.159), channel_id=1, source_target_pairs={{2,0},{4,2},{6,4},{7,6},{5,7},{3,5},{1,3},{0,1},{10,8},{12,10},{14... | collective-permute-start | bytes 884744 | tf_op jit(solution)/shard_map/ppermute | solution.py:338
  212.9 6.1 %collective-permute-start.17 = (bf16[2,576,128]{2,1,0:T(8,128)(2,1)S(1)}, bf16[2,576,128]{2,1,0:T(8,128)(2,1)S(1)}, u32[]{:S(2)}, u32[]{:S(2)}) collective-permute-start(bf16[2,576,128]{2,1,0:T(8,128)(2,1)S(1)} %get-tuple-element.158), channel_id=1, source_target_pairs={{0,2},{2,4},{4,6},{6,7},{7,5},{5,3},{3,1},{1,0},{8,10},{10,12},{12... | collective-permute-start | bytes 884744 | tf_op jit(solution)/shard_map/ppermute | solution.py:338
  213.3 5.9 %collective-permute-start.24 = (bf16[2,576,128]{2,1,0:T(8,128)(2,1)S(1)}, bf16[2,576,128]{2,1,0:T(8,128)(2,1)S(1)}, u32[]{:S(2)}, u32[]{:S(2)}) collective-permute-start(bf16[2,576,128]{2,1,0:T(8,128)(2,1)S(1)} %get-tuple-element.157), channel_id=1, source_target_pairs={{2,0},{4,2},{6,4},{7,6},{5,7},{3,5},{1,3},{0,1},{10,8},{12,10},{14... | collective-permute-start | bytes 884744 | tf_op jit(solution)/shard_map/ppermute | solution.py:338
  220.7 5.6 %collective-permute-start.18 = (bf16[2,576,128]{2,1,0:T(8,128)(2,1)S(1)}, bf16[2,576,128]{2,1,0:T(8,128)(2,1)S(1)}, u32[]{:S(2)}, u32[]{:S(2)}) collective-permute-start(bf16[2,576,128]{2,1,0:T(8,128)(2,1)S(1)} %get-tuple-element.156), channel_id=1, source_target_pairs={{0,2},{2,4},{4,6},{6,7},{7,5},{5,3},{3,1},{1,0},{8,10},{10,12},{12... | collective-permute-start | bytes 884744 | tf_op jit(solution)/shard_map/ppermute | solution.py:338
  221.5 5.6 %collective-permute-start.25 = (bf16[2,576,128]{2,1,0:T(8,128)(2,1)S(1)}, bf16[2,576,128]{2,1,0:T(8,128)(2,1)S(1)}, u32[]{:S(2)}, u32[]{:S(2)}) collective-permute-start(bf16[2,576,128]{2,1,0:T(8,128)(2,1)S(1)} %get-tuple-element.155), channel_id=1, source_target_pairs={{2,0},{4,2},{6,4},{7,6},{5,7},{3,5},{1,3},{0,1},{10,8},{12,10},{14... | collective-permute-start | bytes 884744 | tf_op jit(solution)/shard_map/ppermute | solution.py:338
  228.6 5.6 %collective-permute-start.19 = (bf16[2,576,128]{2,1,0:T(8,128)(2,1)S(1)}, bf16[2,576,128]{2,1,0:T(8,128)(2,1)S(1)}, u32[]{:S(2)}, u32[]{:S(2)}) collective-permute-start(bf16[2,576,128]{2,1,0:T(8,128)(2,1)S(1)} %get-tuple-element.154), channel_id=1, source_target_pairs={{0,2},{2,4},{4,6},{6,7},{7,5},{5,3},{3,1},{1,0},{8,10},{10,12},{12... | collective-permute-start | bytes 884744 | tf_op jit(solution)/shard_map/ppermute | solution.py:338
  230.3 5.6 %collective-permute-start.26 = (bf16[2,576,128]{2,1,0:T(8,128)(2,1)S(1)}, bf16[2,576,128]{2,1,0:T(8,128)(2,1)S(1)}, u32[]{:S(2)}, u32[]{:S(2)}) collective-permute-start(bf16[2,576,128]{2,1,0:T(8,128)(2,1)S(1)} %get-tuple-element.153), channel_id=1, source_target_pairs={{2,0},{4,2},{6,4},{7,6},{5,7},{3,5},{1,3},{0,1},{10,8},{12,10},{14... | collective-permute-start | bytes 884744 | tf_op jit(solution)/shard_map/ppermute | solution.py:338
  237.4 5.8 %collective-permute-start.20 = (bf16[2,576,128]{2,1,0:T(8,128)(2,1)S(1)}, bf16[2,576,128]{2,1,0:T(8,128)(2,1)S(1)}, u32[]{:S(2)}, u32[]{:S(2)}) collective-permute-start(bf16[2,576,128]{2,1,0:T(8,128)(2,1)S(1)} %get-tuple-element.152), channel_id=1, source_target_pairs={{0,2},{2,4},{4,6},{6,7},{7,5},{5,3},{3,1},{1,0},{8,10},{10,12},{12... | collective-permute-start | bytes 884744 | tf_op jit(solution)/shard_map/ppermute | solution.py:338
  238.7 6.0 %collective-permute-start.27 = (bf16[2,576,128]{2,1,0:T(8,128)(2,1)S(1)}, bf16[2,576,128]{2,1,0:T(8,128)(2,1)S(1)}, u32[]{:S(2)}, u32[]{:S(2)}) collective-permute-start(bf16[2,576,128]{2,1,0:T(8,128)(2,1)S(1)} %get-tuple-element.151), channel_id=1, source_target_pairs={{2,0},{4,2},{6,4},{7,6},{5,7},{3,5},{1,3},{0,1},{10,8},{12,10},{14... | collective-permute-start | bytes 884744 | tf_op jit(solution)/shard_map/ppermute | solution.py:338
  246.3 7.4 %collective-permute-start.21 = (bf16[2,576,128]{2,1,0:T(8,128)(2,1)S(1)}, bf16[2,576,128]{2,1,0:T(8,128)(2,1)S(1)}, u32[]{:S(2)}, u32[]{:S(2)}) collective-permute-start(bf16[2,576,128]{2,1,0:T(8,128)(2,1)S(1)} %get-tuple-element.150), channel_id=1, source_target_pairs={{0,2},{2,4},{4,6},{6,7},{7,5},{5,3},{3,1},{1,0},{8,10},{10,12},{12... | collective-permute-start | bytes 884744 | tf_op jit(solution)/shard_map/ppermute | solution.py:338
  247.6 7.9 %collective-permute-start.28 = (bf16[2,576,128]{2,1,0:T(8,128)(2,1)S(1)}, bf16[2,576,128]{2,1,0:T(8,128)(2,1)S(1)}, u32[]{:S(2)}, u32[]{:S(2)}) collective-permute-start(bf16[2,576,128]{2,1,0:T(8,128)(2,1)S(1)} %get-tuple-element.149), channel_id=1, source_target_pairs={{2,0},{4,2},{6,4},{7,6},{5,7},{3,5},{1,3},{0,1},{10,8},{12,10},{14... | collective-permute-start | bytes 884744 | tf_op jit(solution)/shard_map/ppermute | solution.py:338
  257.9 31.0 %copy-start.4 = (bf16[2,576,128]{2,1,0:T(8,128)(2,1)}, bf16[2,576,128]{2,1,0:T(8,128)(2,1)S(1)}, u32[]{:S(2)}) copy-start(bf16[2,576,128]{2,1,0:T(8,128)(2,1)S(1)} %get-tuple-element.148.refs_0_) | copy-start | bytes 884740
  257.9 8.6 %collective-permute-start.29 = (bf16[2,576,128]{2,1,0:T(8,128)(2,1)S(1)}, bf16[2,576,128]{2,1,0:T(8,128)(2,1)S(1)}, u32[]{:S(2)}, u32[]{:S(2)}) collective-permute-start(bf16[2,576,128]{2,1,0:T(8,128)(2,1)S(1)} %get-tuple-element.148.refs_0_), channel_id=1, source_target_pairs={{0,2},{2,4},{4,6},{6,7},{7,5},{5,3},{3,1},{1,0},{8,10},{10,12},{12... | collective-permute-start | bytes 884744 | tf_op jit(solution)/shard_map/ppermute | solution.py:338
  259.7 9.0 %collective-permute-start.30 = (bf16[2,576,128]{2,1,0:T(8,128)(2,1)S(1)}, bf16[2,576,128]{2,1,0:T(8,128)(2,1)S(1)}, u32[]{:S(2)}, u32[]{:S(2)}) collective-permute-start(bf16[2,576,128]{2,1,0:T(8,128)(2,1)S(1)} %get-tuple-element.148.refs_0_), channel_id=1, source_target_pairs={{2,0},{4,2},{6,4},{7,6},{5,7},{3,5},{1,3},{0,1},{10,8},{12,10},{14... | collective-permute-start | bytes 884744 | tf_op jit(solution)/shard_map/ppermute | solution.py:338
  266.5 22.4 %copy-start.5 = (bf16[2,576,128]{2,1,0:T(8,128)(2,1)}, bf16[2,576,128]{2,1,0:T(8,128)(2,1)S(1)}, u32[]{:S(2)}) copy-start(bf16[2,576,128]{2,1,0:T(8,128)(2,1)S(1)} %collective-permute-done.29.refs_1_) | copy-start | bytes 884740
  266.5 5.8 %collective-permute-start.31 = (bf16[2,576,128]{2,1,0:T(8,128)(2,1)S(1)}, bf16[2,576,128]{2,1,0:T(8,128)(2,1)S(1)}, u32[]{:S(2)}, u32[]{:S(2)}) collective-permute-start(bf16[2,576,128]{2,1,0:T(8,128)(2,1)S(1)} %collective-permute-done.29.refs_1_), channel_id=1, source_target_pairs={{0,2},{2,4},{4,6},{6,7},{7,5},{5,3},{3,1},{1,0},{8,10},{10,12},{12... | collective-permute-start | bytes 884744 | tf_op jit(solution)/shard_map/ppermute | solution.py:338
  268.7 20.2 %copy-start.6 = (bf16[2,576,128]{2,1,0:T(8,128)(2,1)}, bf16[2,576,128]{2,1,0:T(8,128)(2,1)S(1)}, u32[]{:S(2)}) copy-start(bf16[2,576,128]{2,1,0:T(8,128)(2,1)S(1)} %collective-permute-done.30.refs_2_) | copy-start | bytes 884740
  268.7 5.6 %collective-permute-start.32 = (bf16[2,576,128]{2,1,0:T(8,128)(2,1)S(1)}, bf16[2,576,128]{2,1,0:T(8,128)(2,1)S(1)}, u32[]{:S(2)}, u32[]{:S(2)}) collective-permute-start(bf16[2,576,128]{2,1,0:T(8,128)(2,1)S(1)} %collective-permute-done.30.refs_2_), channel_id=1, source_target_pairs={{2,0},{4,2},{6,4},{7,6},{5,7},{3,5},{1,3},{0,1},{10,8},{12,10},{14... | collective-permute-start | bytes 884744 | tf_op jit(solution)/shard_map/ppermute | solution.py:338
  272.4 16.6 %copy-start.7 = (bf16[2,576,128]{2,1,0:T(8,128)(2,1)}, bf16[2,576,128]{2,1,0:T(8,128)(2,1)S(1)}, u32[]{:S(2)}) copy-start(bf16[2,576,128]{2,1,0:T(8,128)(2,1)S(1)} %collective-permute-done.31.refs_3_) | copy-start | bytes 884740
  272.4 8.3 %collective-permute-start.33 = (bf16[2,576,128]{2,1,0:T(8,128)(2,1)S(1)}, bf16[2,576,128]{2,1,0:T(8,128)(2,1)S(1)}, u32[]{:S(2)}, u32[]{:S(2)}) collective-permute-start(bf16[2,576,128]{2,1,0:T(8,128)(2,1)S(1)} %collective-permute-done.31.refs_3_), channel_id=1, source_target_pairs={{0,2},{2,4},{4,6},{6,7},{7,5},{5,3},{3,1},{1,0},{8,10},{10,12},{12... | collective-permute-start | bytes 884744 | tf_op jit(solution)/shard_map/ppermute | solution.py:338
  274.3 14.7 %copy-start.8 = (bf16[2,576,128]{2,1,0:T(8,128)(2,1)}, bf16[2,576,128]{2,1,0:T(8,128)(2,1)S(1)}, u32[]{:S(2)}) copy-start(bf16[2,576,128]{2,1,0:T(8,128)(2,1)S(1)} %collective-permute-done.32.refs_4_) | copy-start | bytes 884740
  274.3 7.1 %collective-permute-start.34 = (bf16[2,576,128]{2,1,0:T(8,128)(2,1)S(1)}, bf16[2,576,128]{2,1,0:T(8,128)(2,1)S(1)}, u32[]{:S(2)}, u32[]{:S(2)}) collective-permute-start(bf16[2,576,128]{2,1,0:T(8,128)(2,1)S(1)} %collective-permute-done.32.refs_4_), channel_id=1, source_target_pairs={{2,0},{4,2},{6,4},{7,6},{5,7},{3,5},{1,3},{0,1},{10,8},{12,10},{14... | collective-permute-start | bytes 884744 | tf_op jit(solution)/shard_map/ppermute | solution.py:338
  280.7 8.3 %copy-start.9 = (bf16[2,576,128]{2,1,0:T(8,128)(2,1)}, bf16[2,576,128]{2,1,0:T(8,128)(2,1)S(1)}, u32[]{:S(2)}) copy-start(bf16[2,576,128]{2,1,0:T(8,128)(2,1)S(1)} %collective-permute-done.33.refs_5_) | copy-start | bytes 884740
  280.7 8.2 %collective-permute-start.35 = (bf16[2,576,128]{2,1,0:T(8,128)(2,1)S(1)}, bf16[2,576,128]{2,1,0:T(8,128)(2,1)S(1)}, u32[]{:S(2)}, u32[]{:S(2)}) collective-permute-start(bf16[2,576,128]{2,1,0:T(8,128)(2,1)S(1)} %collective-permute-done.33.refs_5_), channel_id=1, source_target_pairs={{0,2},{2,4},{4,6},{6,7},{7,5},{5,3},{3,1},{1,0},{8,10},{10,12},{12... | collective-permute-start | bytes 884744 | tf_op jit(solution)/shard_map/ppermute | solution.py:338
  281.4 7.6 %copy-start.10 = (bf16[2,576,128]{2,1,0:T(8,128)(2,1)}, bf16[2,576,128]{2,1,0:T(8,128)(2,1)S(1)}, u32[]{:S(2)}) copy-start(bf16[2,576,128]{2,1,0:T(8,128)(2,1)S(1)} %collective-permute-done.34.refs_6_) | copy-start | bytes 884740
  289.0 0.7 copy-start.11
  292.2 0.7 collective-permute-start.36
  296.2 0.7 collective-permute-start.37
  297.6 52.7 %copy-start.1 = (s32[4,5,32]{2,0,1:T(4,128)S(1)}, s32[4,5,32]{2,0,1:T(4,128)}, u32[]{:S(2)}) copy-start(s32[4,5,32]{2,0,1:T(4,128)} %param.10) | copy-start | bytes 7684
  300.3 45.5 %collective-permute-start.38 = (bf16[32,4608]{1,0:T(8,128)(2,1)}, bf16[32,4608]{1,0:T(8,128)(2,1)S(1)}, u32[]{:S(2)}, u32[]{:S(2)}) collective-permute-start(bf16[32,4608]{1,0:T(8,128)(2,1)} %eval_block.6.before), channel_id=1, source_target_pairs={{16,24},{17,25},{18,26},{19,27},{20,28},{21,29},{22,30},{23,31}} | collective-permute-start | bytes 884744 | tf_op jit(solution)/shard_map/ppermute | solution.py:338
  (3 other events, 2.1 us)
